TPU v7x, 32 devices: a whole 2x2x4 slice. The times are simulated.
32 devices in a mesh: ctx: 8 (over y, x, core), fsdp: 4 (over z).
Axes of the slice: x: 2, y: 2, z: 4, core: 2. Of those that a mesh axis runs over, the one named last changes fastest.
Arguments:
- block_in: bfloat16 [4, 2048, 1024], P('fsdp', 'ctx'), may hold values from -6 to 6
- out_grad: bfloat16 [4, 2048, 1024], P('fsdp', 'ctx'), may hold values from -6 to 6
- ln1_gain: bfloat16 [1024], P('fsdp'), may hold values from 0.25 to 1.75
- ln1_shift: bfloat16 [1024], P('fsdp'), may hold values from -4 to 4
- qkv_weight: bfloat16 [1024, 3072], P('fsdp'), may hold values from -0.1875 to 0.1875
- query_bias: bfloat16 [1024], P('fsdp'), may hold values from -4 to 4
- value_bias: bfloat16 [1024], P('fsdp'), may hold values from -4 to 4
- proj_weight: bfloat16 [1024, 1024], P('fsdp'), may hold values from -0.75 to 0.75
- proj_bias: bfloat16 [1024], P('fsdp'), may hold values from -4 to 4
- ln2_gain: bfloat16 [1024], P('fsdp'), may hold values from 0.25 to 1.75
- ln2_shift: bfloat16 [1024], P('fsdp'), may hold values from -4 to 4
- up_weight: bfloat16 [1024, 4096], P('fsdp'), may hold values from -0.1875 to 0.1875
- up_bias: bfloat16 [4096], P('fsdp'), may hold values from -4 to 4
- down_weight: bfloat16 [4096, 1024], P('fsdp'), may hold values from -0.09375 to 0.09375
- down_bias: bfloat16 [1024], P('fsdp'), may hold values from -4 to 4
Outputs:
- block_out: bfloat16 [4, 2048, 1024], P('fsdp', 'ctx')
- d_input: float32 [4, 2048, 1024], P('fsdp', 'ctx')
- d_ln1_gain: float32 [1024], P('fsdp')
- d_ln1_shift: float32 [1024], P('fsdp')
- d_qkv_weight: float32 [1024, 3072], P('fsdp')
- d_query_bias: float32 [1024], P('fsdp')
- d_value_bias: float32 [1024], P('fsdp')
- d_proj_weight: float32 [1024, 1024], P('fsdp')
- d_proj_bias: float32 [1024], P('fsdp')
- d_ln2_gain: float32 [1024], P('fsdp')
- d_ln2_shift: float32 [1024], P('fsdp')
- d_up_weight: float32 [1024, 4096], P('fsdp')
- d_up_bias: float32 [4096], P('fsdp')
- d_down_weight: float32 [4096, 1024], P('fsdp')
- d_down_bias: float32 [1024], P('fsdp')
All inputs are finite; a program needn't handle non-finite values.
Results may differ from a plain program's by a relative error of at most 0.02.
Values may be sent and summed in bfloat16 or wider, within the bound.
No kernel may reach another device: no remote copies, remote signals or barrier semaphores. Data moves between devices by JAX's collectives and lax.ppermute only.
A program may use at most 256 MiB of HBM per device.

v0:
```python
import jax
import jax.numpy as jnp
from jax import lax
from jax.sharding import PartitionSpec as P

HEADS = 16
HEAD_DIM = 64


EPSILON = 1e-05
GELU_COEF = 0.7978845608028654
MASKED = -1e30


def layer_norm(values, gain_vec, shift_vec):
    center = values - jnp.mean(values, -1, keepdims=True)
    spread = jnp.mean(center * center, -1, keepdims=True)
    return center * lax.rsqrt(spread + EPSILON) * gain_vec + shift_vec


def gelu_tanh(values):
    return (
        0.5 * values * (1.0 + jnp.tanh(GELU_COEF * (values + 0.044715 * values * values * values)))
    )


def contract_rows(left, right):
    return lax.dot_general(
        left, right, (((0,), (0,)), ((), ())), preferred_element_type=jnp.float32
    )


def times_trans(left, right):
    return lax.dot_general(
        left, right, (((1,), (1,)), ((), ())), preferred_element_type=jnp.float32
    )


def shards(
    block_in,
    out_grad,
    ln1_gain,
    ln1_shift,
    qkv_weight,
    query_bias,
    value_bias,
    proj_weight,
    proj_bias,
    ln2_gain,
    ln2_shift,
    up_weight,
    up_bias,
    down_weight,
    down_bias,
):
    seq_count, blk_len, model_dim = block_in.shape
    tok_count = seq_count * blk_len
    attn_scale = HEAD_DIM ** (-0.5)
    cycle_size = lax.axis_size("ctx")
    cycle_index = lax.axis_index("ctx")
    gathered = (
        lax.all_gather(ln1_gain, "fsdp", axis=0, tiled=True),
        lax.all_gather(ln1_shift, "fsdp", axis=0, tiled=True),
        lax.all_gather(qkv_weight, "fsdp", axis=0, tiled=True),
        lax.all_gather(query_bias, "fsdp", axis=0, tiled=True),
        lax.all_gather(value_bias, "fsdp", axis=0, tiled=True),
        lax.all_gather(proj_weight, "fsdp", axis=0, tiled=True),
        lax.all_gather(proj_bias, "fsdp", axis=0, tiled=True),
        lax.all_gather(ln2_gain, "fsdp", axis=0, tiled=True),
        lax.all_gather(ln2_shift, "fsdp", axis=0, tiled=True),
        lax.all_gather(up_weight, "fsdp", axis=0, tiled=True),
        lax.all_gather(up_bias, "fsdp", axis=0, tiled=True),
        lax.all_gather(down_weight, "fsdp", axis=0, tiled=True),
        lax.all_gather(down_bias, "fsdp", axis=0, tiled=True),
    )
    gain_one = gathered[0].astype(jnp.float32)
    shift_one = gathered[1].astype(jnp.float32)
    qkv_full = gathered[2]
    qbias_full = gathered[3].astype(jnp.float32)
    vbias_full = gathered[4].astype(jnp.float32)
    proj_full = gathered[5]
    pbias_full = gathered[6].astype(jnp.float32)
    gain_two = gathered[7].astype(jnp.float32)
    shift_two = gathered[8].astype(jnp.float32)
    up_full = gathered[9]
    ubias_full = gathered[10].astype(jnp.float32)
    down_full = gathered[11]
    dbias_full = gathered[12].astype(jnp.float32)
    inputs_f = block_in.reshape(tok_count, model_dim).astype(jnp.float32)
    normed_low = layer_norm(inputs_f, gain_one, shift_one).astype(jnp.bfloat16)
    projected = jnp.dot(normed_low, qkv_full, preferred_element_type=jnp.float32)
    queries = (
        (projected[:, :model_dim] + qbias_full)
        .astype(jnp.bfloat16)
        .reshape(seq_count, blk_len, HEADS, HEAD_DIM)
    )
    keys_own = (
        projected[:, model_dim : 2 * model_dim]
        .astype(jnp.bfloat16)
        .reshape(seq_count, blk_len, model_dim)
    )
    values_own = (
        (projected[:, 2 * model_dim :] + vbias_full)
        .astype(jnp.bfloat16)
        .reshape(seq_count, blk_len, model_dim)
    )
    query_pos = cycle_index * blk_len + jnp.arange(blk_len, dtype=jnp.int32)

    def block_scores(key_blk, key_start):
        key_heads = key_blk.reshape(seq_count, blk_len, HEADS, HEAD_DIM)
        scores = (
            jnp.einsum("sqhd,skhd->sqhk", queries, key_heads, preferred_element_type=jnp.float32)
            * attn_scale
        )
        key_pos = key_start + jnp.arange(blk_len, dtype=jnp.int32)
        allowed = (key_pos[None, :] <= query_pos[:, None])[None, :, None, :]
        return (jnp.where(allowed, scores, MASKED), allowed)

    start_state = (
        jnp.full((seq_count, blk_len, HEADS), MASKED, jnp.float32),
        jnp.zeros((seq_count, blk_len, HEADS), jnp.float32),
        jnp.zeros((seq_count, blk_len, HEADS, HEAD_DIM), jnp.float32),
    )
    keys_in = lax.all_gather(keys_own, "ctx", axis=1, tiled=True)
    values_in = lax.all_gather(values_own, "ctx", axis=1, tiled=True)
    block_total = keys_in.shape[1] // blk_len

    def visit(number, state):
        run_max, run_sum, run_acc = state
        key_blk = lax.dynamic_slice_in_dim(keys_in, number * blk_len, blk_len, 1)
        val_blk = lax.dynamic_slice_in_dim(values_in, number * blk_len, blk_len, 1)
        scores, allowed = block_scores(key_blk, number * blk_len)
        new_max = jnp.maximum(run_max, jnp.max(scores, -1))
        weights = jnp.where(allowed, jnp.exp(scores - new_max[..., None]), 0.0)
        factor = jnp.exp(run_max - new_max)
        new_sum = run_sum * factor + jnp.sum(weights, -1)
        val_heads = val_blk.reshape(seq_count, blk_len, HEADS, HEAD_DIM)
        new_acc = run_acc * factor[..., None] + jnp.einsum(
            "sqhk,skhd->sqhd",
            weights.astype(jnp.bfloat16),
            val_heads,
            preferred_element_type=jnp.float32,
        )
        return (new_max, new_sum, new_acc)

    run_max, run_sum, run_acc = lax.fori_loop(0, block_total, visit, start_state)
    log_total = run_max + jnp.log(run_sum)
    attn_out = run_acc / run_sum[..., None]
    attn_low = attn_out.reshape(tok_count, model_dim).astype(jnp.bfloat16)
    resid_one = (
        inputs_f + jnp.dot(attn_low, proj_full, preferred_element_type=jnp.float32) + pbias_full
    )
    normed_two_low = layer_norm(resid_one, gain_two, shift_two).astype(jnp.bfloat16)
    pre_act = jnp.dot(normed_two_low, up_full, preferred_element_type=jnp.float32) + ubias_full
    hidden_low = gelu_tanh(pre_act).astype(jnp.bfloat16)
    final_rows = (
        resid_one + jnp.dot(hidden_low, down_full, preferred_element_type=jnp.float32) + dbias_full
    )
    block_out = final_rows.astype(jnp.bfloat16).reshape(seq_count, blk_len, model_dim)
    grad_low = out_grad.reshape(tok_count, model_dim)
    grad_f = grad_low.astype(jnp.float32)
    d_down = contract_rows(hidden_low, grad_low)
    d_dbias = jnp.sum(grad_f, 0)
    d_hidden = times_trans(grad_low, down_full)
    gelu_out, gelu_pull = jax.vjp(gelu_tanh, pre_act)
    d_pre = gelu_pull(d_hidden)[0].astype(jnp.bfloat16)
    d_up = contract_rows(normed_two_low, d_pre)
    d_ubias = jnp.sum(d_pre.astype(jnp.float32), 0)
    d_normed_two = times_trans(d_pre, up_full)
    norm_two_out, norm_two_pull = jax.vjp(layer_norm, resid_one, gain_two, shift_two)
    d_resid_part, d_gain_two, d_shift_two = norm_two_pull(d_normed_two)
    d_resid = grad_f + d_resid_part
    d_branch_low = d_resid.astype(jnp.bfloat16)
    d_proj = contract_rows(attn_low, d_branch_low)
    d_pbias = jnp.sum(d_branch_low.astype(jnp.float32), 0)
    d_attn_low = (
        times_trans(d_branch_low, proj_full)
        .astype(jnp.bfloat16)
        .reshape(seq_count, blk_len, HEADS, HEAD_DIM)
    )
    row_delta = jnp.sum(d_attn_low.astype(jnp.float32) * attn_out, -1)

    def block_grads(key_blk, val_blk, key_start, d_query):
        scores, allowed = block_scores(key_blk, key_start)
        probs = jnp.where(allowed, jnp.exp(scores - log_total[..., None]), 0.0)
        key_heads = key_blk.reshape(seq_count, blk_len, HEADS, HEAD_DIM)
        val_heads = val_blk.reshape(seq_count, blk_len, HEADS, HEAD_DIM)
        d_val = jnp.einsum(
            "sqhk,sqhd->skhd",
            probs.astype(jnp.bfloat16),
            d_attn_low,
            preferred_element_type=jnp.float32,
        )
        d_prob = jnp.einsum(
            "sqhd,skhd->sqhk", d_attn_low, val_heads, preferred_element_type=jnp.float32
        )
        d_score = (probs * (d_prob - row_delta[..., None])).astype(jnp.bfloat16)
        d_query = (
            d_query
            + jnp.einsum("sqhk,skhd->sqhd", d_score, key_heads, preferred_element_type=jnp.float32)
            * attn_scale
        )
        d_key = (
            jnp.einsum("sqhk,sqhd->skhd", d_score, queries, preferred_element_type=jnp.float32)
            * attn_scale
        )
        return (
            d_query,
            d_key.reshape(seq_count, blk_len, model_dim),
            d_val.reshape(seq_count, blk_len, model_dim),
        )

    zero_query = jnp.zeros((seq_count, blk_len, HEADS, HEAD_DIM), jnp.float32)
    keys_all, values_all = (
        lax.all_gather(keys_own, "ctx", axis=1, tiled=True),
        lax.all_gather(values_own, "ctx", axis=1, tiled=True),
    )
    zero_whole = jnp.zeros((seq_count, blk_len * cycle_size, model_dim), jnp.float32)

    def visit_back(number, state):
        d_keys_all, d_values_all, d_query = state
        key_blk = lax.dynamic_slice_in_dim(keys_all, number * blk_len, blk_len, 1)
        val_blk = lax.dynamic_slice_in_dim(values_all, number * blk_len, blk_len, 1)
        d_query, d_key_blk, d_val_blk = block_grads(key_blk, val_blk, number * blk_len, d_query)
        d_keys_all = lax.dynamic_update_slice_in_dim(d_keys_all, d_key_blk, number * blk_len, 1)
        d_values_all = lax.dynamic_update_slice_in_dim(d_values_all, d_val_blk, number * blk_len, 1)
        return (d_keys_all, d_values_all, d_query)

    d_keys_all, d_values_all, d_query_all = lax.fori_loop(
        0, cycle_size, visit_back, (zero_whole, zero_whole, zero_query)
    )
    d_keys, d_values = (
        lax.psum_scatter(
            d_keys_all.astype(jnp.bfloat16), "ctx", scatter_dimension=1, tiled=True
        ).astype(jnp.float32),
        lax.psum_scatter(
            d_values_all.astype(jnp.bfloat16), "ctx", scatter_dimension=1, tiled=True
        ).astype(jnp.float32),
    )
    d_query_low = d_query_all.reshape(tok_count, model_dim).astype(jnp.bfloat16)
    d_value_low = d_values.reshape(tok_count, model_dim).astype(jnp.bfloat16)
    d_qkv = jnp.concatenate(
        [d_query_low, d_keys.reshape(tok_count, model_dim).astype(jnp.bfloat16), d_value_low], 1
    )
    d_qkv_full = contract_rows(normed_low, d_qkv)
    d_qbias = jnp.sum(d_query_low.astype(jnp.float32), 0)
    d_vbias = jnp.sum(d_value_low.astype(jnp.float32), 0)
    d_normed_one = times_trans(d_qkv, qkv_full)
    norm_one_out, norm_one_pull = jax.vjp(layer_norm, inputs_f, gain_one, shift_one)
    d_in_part, d_gain_one, d_shift_one = norm_one_pull(d_normed_one)
    d_input = (d_resid + d_in_part).reshape(seq_count, blk_len, model_dim)
    summed = (
        lax.psum_scatter(
            d_gain_one.astype(jnp.bfloat16), "fsdp", scatter_dimension=0, tiled=True
        ).astype(jnp.float32),
        lax.psum_scatter(
            d_shift_one.astype(jnp.bfloat16), "fsdp", scatter_dimension=0, tiled=True
        ).astype(jnp.float32),
        lax.psum_scatter(
            d_qkv_full.astype(jnp.bfloat16), "fsdp", scatter_dimension=0, tiled=True
        ).astype(jnp.float32),
        lax.psum_scatter(
            d_qbias.astype(jnp.bfloat16), "fsdp", scatter_dimension=0, tiled=True
        ).astype(jnp.float32),
        lax.psum_scatter(
            d_vbias.astype(jnp.bfloat16), "fsdp", scatter_dimension=0, tiled=True
        ).astype(jnp.float32),
        lax.psum_scatter(
            d_proj.astype(jnp.bfloat16), "fsdp", scatter_dimension=0, tiled=True
        ).astype(jnp.float32),
        lax.psum_scatter(
            d_pbias.astype(jnp.bfloat16), "fsdp", scatter_dimension=0, tiled=True
        ).astype(jnp.float32),
        lax.psum_scatter(
            d_gain_two.astype(jnp.bfloat16), "fsdp", scatter_dimension=0, tiled=True
        ).astype(jnp.float32),
        lax.psum_scatter(
            d_shift_two.astype(jnp.bfloat16), "fsdp", scatter_dimension=0, tiled=True
        ).astype(jnp.float32),
        lax.psum_scatter(d_up.astype(jnp.bfloat16), "fsdp", scatter_dimension=0, tiled=True).astype(
            jnp.float32
        ),
        lax.psum_scatter(
            d_ubias.astype(jnp.bfloat16), "fsdp", scatter_dimension=0, tiled=True
        ).astype(jnp.float32),
        lax.psum_scatter(
            d_down.astype(jnp.bfloat16), "fsdp", scatter_dimension=0, tiled=True
        ).astype(jnp.float32),
        lax.psum_scatter(
            d_dbias.astype(jnp.bfloat16), "fsdp", scatter_dimension=0, tiled=True
        ).astype(jnp.float32),
    )
    totals = (
        lax.psum(summed[0].astype(jnp.bfloat16), "ctx").astype(jnp.float32),
        lax.psum(summed[1].astype(jnp.bfloat16), "ctx").astype(jnp.float32),
        lax.psum(summed[2].astype(jnp.bfloat16), "ctx").astype(jnp.float32),
        lax.psum(summed[3].astype(jnp.bfloat16), "ctx").astype(jnp.float32),
        lax.psum(summed[4].astype(jnp.bfloat16), "ctx").astype(jnp.float32),
        lax.psum(summed[5].astype(jnp.bfloat16), "ctx").astype(jnp.float32),
        lax.psum(summed[6].astype(jnp.bfloat16), "ctx").astype(jnp.float32),
        lax.psum(summed[7].astype(jnp.bfloat16), "ctx").astype(jnp.float32),
        lax.psum(summed[8].astype(jnp.bfloat16), "ctx").astype(jnp.float32),
        lax.psum(summed[9].astype(jnp.bfloat16), "ctx").astype(jnp.float32),
        lax.psum(summed[10].astype(jnp.bfloat16), "ctx").astype(jnp.float32),
        lax.psum(summed[11].astype(jnp.bfloat16), "ctx").astype(jnp.float32),
        lax.psum(summed[12].astype(jnp.bfloat16), "ctx").astype(jnp.float32),
    )
    return (
        block_out,
        d_input,
        totals[0],
        totals[1],
        totals[2],
        totals[3],
        totals[4],
        totals[5],
        totals[6],
        totals[7],
        totals[8],
        totals[9],
        totals[10],
        totals[11],
        totals[12],
    )


def solution(mesh):
    in_specs = (
        P("fsdp", "ctx", None),
        P("fsdp", "ctx", None),
        P("fsdp"),
        P("fsdp"),
        P("fsdp", None),
        P("fsdp"),
        P("fsdp"),
        P("fsdp", None),
        P("fsdp"),
        P("fsdp"),
        P("fsdp"),
        P("fsdp", None),
        P("fsdp"),
        P("fsdp", None),
        P("fsdp"),
    )
    out_specs = (
        P("fsdp", "ctx", None),
        P("fsdp", "ctx", None),
        P("fsdp"),
        P("fsdp"),
        P("fsdp", None),
        P("fsdp"),
        P("fsdp"),
        P("fsdp", None),
        P("fsdp"),
        P("fsdp"),
        P("fsdp"),
        P("fsdp", None),
        P("fsdp"),
        P("fsdp", None),
        P("fsdp"),
    )
    return jax.shard_map(shards, mesh=mesh, in_specs=in_specs, out_specs=out_specs, check_vma=False)
```

profile of v0, /device:TPU:0, one launch (start us, length us, event | category | flops | bytes accessed | tf_op | source)
XLA Modules:
  0.0 1331.6 jit_solution(14812793287742140914)
XLA Ops:
  10.6 12.6 all-gather.5
  23.2 7.7 all-gather.4
  30.9 11.3 all-gather.3
  42.2 8.5 all-gather.2
  53.3 74.5 %all-gather.17.cloned.1.call-done = bf16[1024,3072]{1,0:T(8,128)(2,1)} async-done(((bf16[256,3072]{1,0:T(8,128)(2,1)}), bf16[1024,3072]{1,0:T(8,128)(2,1)}) %all-gather.17.cloned.1.call-update) | async-done | bytes 6291472 | tf_op jit(solution)/shard_map/all_gather | solution.py:64
  127.8 4.9 fusion.94
  136.8 7.9 all-gather.8
  144.7 9.3 all-gather.7
  154.0 7.9 all-gather.6
  161.9 12.4 all_gather.59
  174.5 6.5 copy.58
  181.0 27.3 %all-gather.25.cloned.1.call-done = bf16[2048,1024]{1,0:T(8,128)(2,1)} async-done(((bf16[256,1024]{1,0:T(8,128)(2,1)}), bf16[2048,1024]{1,0:T(8,128)(2,1)}) %all-gather.25.cloned.1.call-update) | async-done | bytes 4194320 | tf_op jit(solution)/shard_map/all_gather | solution.py:124
  208.2 6.4 copy.57
  214.7 44.3 %while.36 = (s32[]{:T(128)}, f32[1,256,16]{1,2,0:T(8,128)S(1)}, f32[1,256,16]{1,2,0:T(8,128)S(1)}, f32[1,256,16,64]{1,3,2,0:T(8,128)}, bf16[1,2048,1024]{1,2,0:T...) while((s32[]{:T(128)}, f32[1,256,16]{1,2,0:T(8,128)S(1)}, ...), condition=%wide.region_5.6_spmd.clone, body=%wide.region_2.5_spmd.clone.sunk | while | flops 282944000 | bytes 27267324 | solution.py:146
  259.0 2.1 fusion.88
  261.1 2.9 fusion.102
  264.3 141.1 %all-gather.21.cloned.1.call-done = bf16[1024,4096]{1,0:T(8,128)(2,1)} async-done(((bf16[256,4096]{1,0:T(8,128)(2,1)}), bf16[1024,4096]{1,0:T(8,128)(2,1)}) %all-gather.21.cloned.1.call-update) | async-done | bytes 8388624 | tf_op jit(solution)/shard_map/all_gather | solution.py:71
  405.4 7.8 convolution_add_fusion
  413.3 141.5 %all-gather.23.cloned.1.call-done = bf16[4096,1024]{1,0:T(8,128)(2,1)} async-done(((bf16[1024,1024]{1,0:T(8,128)(2,1)}), bf16[4096,1024]{1,0:T(8,128)(2,1)}) %all-gather.23.cloned.1.call-update) | async-done | bytes 8388624 | tf_op jit(solution)/shard_map/all_gather | solution.py:73
  554.8 9.0 fusion.103
  563.8 2.6 multiply_reduce_fusion
  570.4 2.1 copy.59
  574.1 2.5 broadcast_in_dim.139.clone
  576.6 2.5 broadcast_in_dim.139
  579.1 65.8 %while.37 = (s32[]{:T(128)}, bf16[1,2048,1024]{1,2,0:T(8,128)(2,1)}, bf16[1,2048,1024]{1,2,0:T(8,128)(2,1)}, f32[1,256,16,64]{1,3,2,0:T(8,128)S(1)}, bf16[1,2048...) while((s32[]{:T(128)}, ...), condition=%wide.region_12.13_spmd.clone, body=%wide.region_11.12_spmd.clone.sunk | while | flops 685048320 | bytes 32231676 | solution.py:229
  608.0 1.6 fusion.164
  624.5 1.6 fusion.164
  640.9 1.6 fusion.164
  645.7 3.2 convolution_convert_fusion.3
  649.2 8.8 convolution_convert_fusion
  658.1 7.3 convolution_convert_fusion.1
  666.4 28.3 %reduce-scatter.7.cloned.1.call-done = bf16[1,256,1024]{1,2,0:T(8,128)(2,1)} async-done(((bf16[1,2048,1024]{1,2,0:T(8,128)(2,1)}), bf16[1,256,1024]{1,2,0:T(8,128)(2,1)}) %reduce-scatter.7.cloned.1.call-update) | async-done | bytes 524304 | tf_op jit(solution)/shard_map/reduce_scatter | solution.py:233
  694.7 55.1 %reduce-scatter.9.cloned.1.call-done = bf16[1,256,1024]{1,2,0:T(8,128)(2,1)} async-done(((bf16[1,2048,1024]{1,2,0:T(8,128)(2,1)}), bf16[1,256,1024]{1,2,0:T(8,128)(2,1)}) %reduce-scatter.9.cloned.1.call-update) | async-done | bytes 524304 | tf_op jit(solution)/shard_map/reduce_scatter | solution.py:236
  749.8 6.1 convolution_convert_fusion.2
  756.0 40.5 %reduce-scatter.13.cloned.1.call-done = bf16[256,1024]{1,0:T(8,128)(2,1)} async-done(((bf16[1024,1024]{1,0:T(8,128)(2,1)}), bf16[256,1024]{1,0:T(8,128)(2,1)}) %reduce-scatter.13.cloned.1.call-update) | async-done | bytes 524304 | tf_op jit(solution)/shard_map/reduce_scatter | solution.py:268
  796.5 146.1 %reduce-scatter.17.cloned.1.call-done = bf16[1024,1024]{1,0:T(8,128)(2,1)} async-done(((bf16[4096,1024]{1,0:T(8,128)(2,1)}), bf16[1024,1024]{1,0:T(8,128)(2,1)}) %reduce-scatter.17.cloned.1.call-update) | async-done | bytes 2097168 | tf_op jit(solution)/shard_map/reduce_scatter | solution.py:286
  942.7 147.7 %reduce-scatter.15.cloned.1.call-done = bf16[256,4096]{1,0:T(8,128)(2,1)} async-done(((bf16[1024,4096]{1,0:T(8,128)(2,1)}), bf16[256,4096]{1,0:T(8,128)(2,1)}) %reduce-scatter.15.cloned.1.call-update) | async-done | bytes 2097168 | tf_op jit(solution)/shard_map/reduce_scatter | solution.py:280
  1090.4 113.8 %reduce-scatter.11.cloned.1.call-done = bf16[256,3072]{1,0:T(8,128)(2,1)} async-done(((bf16[1024,3072]{1,0:T(8,128)(2,1)}), bf16[256,3072]{1,0:T(8,128)(2,1)}) %reduce-scatter.11.cloned.1.call-update) | async-done | bytes 1572880 | tf_op jit(solution)/shard_map/reduce_scatter | solution.py:259
  1206.2 10.4 all-gather.9
  1216.7 8.4 fusion.71
  1225.3 5.5 fusion.97
  1231.3 16.7 %all-reduce.11 = (bf16[1024]{0:T(1024)(128)(2,1)S(1)}, bf16[1024]{0:T(1024)(128)(2,1)S(1)}, bf16[1024]{0:T(1024)(128)(2,1)S(1)}, bf16[1024]{0:T(1024)(128)(2,1)S...) all-reduce(bf16[1024]{0:T(1024)(128)(2,1)S(1)} %get-tuple-element.4, ...), channel_id=6, replica_groups=mesh['ctx'=8,'fsdp'=4] {'fsdp'}, use_global_device_ids=true, to_apply=%region_18.19.clone | all-reduce | flops 12288 | bytes 49152
  1248.6 12.5 all-reduce.9
  1267.7 46.3 %all-reduce.14.cloned.1.call-done = (bf16[256,3072]{1,0:T(8,128)(2,1)}, bf16[256,1024]{1,0:T(8,128)(2,1)}, bf16[256,4096]{1,0:T(8,128)(2,1)}, bf16[1024,1024]{1,0:T(8,128)(2,1)}) async-done(((bf16[256,3072]{1,0:T(8,128)(2,1)}, bf16[256,1024]{1,0:T(8,128)(2,1)}, bf16[256,4096]{1,0:T(8,128)(2,1)}, bf16[1024,1024]{1,0:T(8,128)(2,1)}), (bf16[256,3072]{1,0:T(8,128)(2,1)}, bf16[256,1024]{1,0:T(8,128)(2,1)}, ...) | async-done | bytes 6291472 | tf_op jit(solution)/shard_map/psum | solution.py:296
  1314.1 2.3 convert_element_type.262
  1316.4 3.4 convert_element_type.258
  1319.8 2.5 convert_element_type.269
  1322.3 2.5 convert_element_type.272
  (340 shorter events, 131.1 us)
Async XLA Ops:
  7.2 120.7 %all-gather.17.cloned.1.call-start = ((), (), s32[]{:S(2)}) async-start(), calls=%async_computation.6 | async-start | bytes 7864320 | tf_op jit(solution)/shard_map/all_gather | solution.py:64
  7.9 166.6 %all-gather.27.cloned.1.call-start = ((), (), s32[]{:S(2)}) async-start(), calls=%async_computation.17 | async-start | bytes 4718592 | tf_op jit(solution)/shard_map/all_gather | solution.py:125
  53.3 79.4 %copy-start.15 = (f32[256]{0:T(256)}, f32[256]{0:T(256)S(1)}, u32[]{:S(2)}) copy-start(f32[256]{0:T(256)S(1)} %fusion.77) | copy-start | bytes 3076
  134.0 2.8 copy-start.19
  134.0 2.8 copy-start.20
  134.0 2.9 copy-start.21
  134.0 27.9 %copy-start.17 = (bf16[1024]{0:T(1024)(128)(2,1)S(1)}, bf16[1024]{0:T(1024)(128)(2,1)}, u32[]{:S(2)}) copy-start(bf16[1024]{0:T(1024)(128)(2,1)} %param.31) | copy-start | bytes 6148
  134.0 74.2 %all-gather.25.cloned.1.call-start = ((), (), s32[]{:S(2)}) async-start(), calls=%async_computation.16 | async-start | bytes 4718592 | tf_op jit(solution)/shard_map/all_gather | solution.py:124
  134.9 39.4 %copy-start.13 = (bf16[256,1024]{1,0:T(8,128)(2,1)S(1)}, bf16[256,1024]{1,0:T(8,128)(2,1)}, u32[]{:S(2)}) copy-start(bf16[256,1024]{1,0:T(8,128)(2,1)} %get-tuple-element.558) | copy-start | bytes 1572868
  134.9 126.2 %all-gather.19.cloned.1.call-start = ((), (), s32[]{:S(2)}) async-start(), calls=%async_computation.7 | async-start | bytes 2621440 | tf_op jit(solution)/shard_map/all_gather | solution.py:67
  135.5 269.9 %all-gather.21.cloned.1.call-start = ((), (), s32[]{:S(2)}) async-start(), calls=%async_computation.8 | async-start | bytes 10485760 | tf_op jit(solution)/shard_map/all_gather | solution.py:71
  136.1 418.7 %all-gather.23.cloned.1.call-start = ((), (), s32[]{:S(2)}) async-start(), calls=%async_computation.9 | async-start | bytes 10485760 | tf_op jit(solution)/shard_map/all_gather | solution.py:73
  136.7 558.0 %reduce-scatter.7.cloned.1.call-start = ((), (), s32[]{:S(2)}) async-start(), calls=%async_computation.10 | async-start | bytes 4718592 | tf_op jit(solution)/shard_map/reduce_scatter | solution.py:233
  214.7 46.4 %copy-start = (bf16[1,256,1024]{2,1,0:T(8,128)(2,1)S(1)}, bf16[1,256,1024]{2,1,0:T(8,128)(2,1)}, u32[]{:S(2)}) copy-start(bf16[1,256,1024]{2,1,0:T(8,128)(2,1)} %param.19) | copy-start | bytes 1572868
  216.1 1.9 copy-start.5
  221.7 1.9 copy-start.5
  227.2 1.9 copy-start.5
  232.7 1.9 copy-start.5
  238.3 1.9 copy-start.5
  243.8 1.9 copy-start.5
  249.3 1.9 copy-start.5
  254.9 1.9 copy-start.5
  554.8 9.0 copy-start.18
  563.7 2.7 copy-start.7
  563.8 4.1 copy-start.3
  566.4 2.5 copy-start.10
  579.1 3.1 copy-start.11
  587.3 3.1 copy-start.11
  595.5 3.1 copy-start.11
  603.8 3.1 copy-start.11
  612.0 3.1 copy-start.11
  620.2 3.1 copy-start.11
  628.4 3.1 copy-start.11
  636.7 3.1 copy-start.11
  644.9 104.9 %reduce-scatter.9.cloned.1.call-start = ((), (), s32[]{:S(2)}) async-start(), calls=%async_computation.11 | async-start | bytes 4718592 | tf_op jit(solution)/shard_map/reduce_scatter | solution.py:236
  645.0 4.3 copy-start.4
  645.7 150.9 %reduce-scatter.13.cloned.1.call-start = ((), (), s32[]{:S(2)}) async-start(), calls=%async_computation.13 | async-start | bytes 2621440 | tf_op jit(solution)/shard_map/reduce_scatter | solution.py:268
  649.0 293.7 %reduce-scatter.17.cloned.1.call-start = ((), (), s32[]{:S(2)}) async-start(), calls=%async_computation.15 | async-start | bytes 10485760 | tf_op jit(solution)/shard_map/reduce_scatter | solution.py:286
  658.0 432.3 %reduce-scatter.15.cloned.1.call-start = ((), (), s32[]{:S(2)}) async-start(), calls=%async_computation.14 | async-start | bytes 10485760 | tf_op jit(solution)/shard_map/reduce_scatter | solution.py:280
  665.5 538.7 %reduce-scatter.11.cloned.1.call-start = ((), (), s32[]{:S(2)}) async-start(), calls=%async_computation.12 | async-start | bytes 7864320 | tf_op jit(solution)/shard_map/reduce_scatter | solution.py:259
  755.9 448.3 %copy-start.23 = (u32[32]{0:T(128)S(1)}, u32[32]{0:T(128)}, u32[]{:S(2)}) copy-start(u32[32]{0:T(128)} %constant.148) | copy-start | bytes 388
  755.9 450.2 %copy-start.22 = (bf16[256]{0:T(256)(128)(2,1)S(1)}, bf16[256]{0:T(256)(128)(2,1)}, u32[]{:S(2)}) copy-start(bf16[256]{0:T(256)(128)(2,1)} %param.33) | copy-start | bytes 1540
  755.9 558.2 %all-reduce.14.cloned.1.call-start = ((), (), s32[]{:S(2)}) async-start(), calls=%async_computation.18 | async-start | bytes 12582912 | tf_op jit(solution)/shard_map/psum | solution.py:296
  1216.7 8.4 copy-start.14
  1225.3 5.5 copy-start.16
  1225.3 41.0 %copy-start.2 = (f32[256,1024]{1,0:T(8,128)S(1)}, f32[256,1024]{1,0:T(8,128)}, u32[]{:S(2)}) copy-start(f32[256,1024]{1,0:T(8,128)} %copy-done.1) | copy-start | bytes 3145732
  1314.1 5.7 copy-start.9
  1319.8 2.5 copy-start.8
  (10 other events, 9.6 us)
Sparse Core Ops, SparseCore 0:
  9.6 118.2 all-gather.16
  134.1 34.8 all-gather.26
  171.5 36.7 all-gather.24
  209.7 45.9 all-gather.18
  257.1 148.3 all-gather.20
  406.9 147.8 all-gather.22
  645.0 49.5 reduce-scatter.6
  698.4 51.3 reduce-scatter.8
  752.6 43.8 reduce-scatter.12
  798.8 143.7 reduce-scatter.16
  945.2 145.1 reduce-scatter.14
  1092.6 111.4 reduce-scatter.10
  1208.2 105.8 all-reduce.13
where the time goes:
time: 1340 us; the launch traced here: 1330 us
  waiting for transfers between devices  965 us (72%)
  matrix products  123 us (9%)
  blocking collectives  117 us (9%)
  local copies, waits for them, and re-layouts  71.3 us (5%)
  other arithmetic  37.4 us (3%)
  between operations  15.9 us (1%)
    reduce_scatter x1, waiting for transfers between devices, shards(): lax.psum_scatter(d_up.astype(jnp.bfloat16), 'fsdp', scatter_dimension=0,...  148 us
    reduce_scatter x1, waiting for transfers between devices, shards(): lax.psum_scatter(d_down.astype(jnp.bfloat16), 'fsdp', scatter_dimension=0...  146 us
    all_gather x1, waiting for transfers between devices, shards(): lax.all_gather(down_weight, 'fsdp', axis=0, tiled=True)  141 us
    all_gather x1, waiting for transfers between devices, shards(): lax.all_gather(up_weight, 'fsdp', axis=0, tiled=True)  141 us
    reduce_scatter x1, waiting for transfers between devices, shards(): lax.psum_scatter(d_qkv_full.astype(jnp.bfloat16), 'fsdp', scatter_dimensi...  114 us
    all_gather x1, waiting for transfers between devices, shards(): lax.all_gather(qkv_weight, 'fsdp', axis=0, tiled=True)  74.5 us
    reduce_scatter x1, waiting for transfers between devices, shards(): lax.psum_scatter(d_values_all.astype(jnp.bfloat16), 'ctx', scatter_dimens...  55.1 us
    psum x1, waiting for transfers between devices, shards(): lax.psum(summed[2].astype(jnp.bfloat16), 'ctx').astype(jnp.float32)  46.3 us
  transfers between devices with their start and end apart: 13, of which 11 were waited for; matrix products, arithmetic and copies ran while one was open for 9% of the time, Pallas kernels for 0%

commit v1 on v0

v1 whole, which is shorter than its diff:
```python
import functools
import math

import jax
import jax.numpy as jnp
from jax import lax
from jax.experimental import pallas as pl
from jax.experimental.pallas import tpu as pltpu
from jax.sharding import PartitionSpec as P

HEADS = 16
HEAD_DIM = 64

EPSILON = 1e-05
GELU_COEF = 0.7978845608028654
MASKED = -1e30
SCORE_SCALE = HEAD_DIM ** (-0.5)
EXP2_SCALE = SCORE_SCALE / math.log(2.0)
F32 = jnp.float32
BF16 = jnp.bfloat16


def layer_norm(values, gain_vec, shift_vec):
    center = values - jnp.mean(values, -1, keepdims=True)
    spread = jnp.mean(center * center, -1, keepdims=True)
    return center * lax.rsqrt(spread + EPSILON) * gain_vec + shift_vec


def gelu_tanh(values):
    return (
        0.5 * values * (1.0 + jnp.tanh(GELU_COEF * (values + 0.044715 * values * values * values)))
    )


def contract_rows(left, right):
    return lax.dot_general(left, right, (((0,), (0,)), ((), ())), preferred_element_type=F32)


def times_trans(left, right):
    return lax.dot_general(left, right, (((1,), (1,)), ((), ())), preferred_element_type=F32)


def times(left, right):
    return jnp.dot(left, right, preferred_element_type=F32)


def ctx_swap(value, bits):
    size = lax.axis_size("ctx")
    return lax.ppermute(value, "ctx", [(at, at ^ bits) for at in range(size)])


def ctx_base():
    return lax.axis_index("ctx") if lax.axis_size("ctx") == 8 else jnp.int32(0)


def ctx_gather(block):
    if lax.axis_size("ctx") != 8:
        return lax.all_gather(block, "ctx", axis=0)
    half = block.shape[0] // 2
    by_x = ctx_swap(block, 2)
    by_y = ctx_swap(block, 4)
    own_pair = ctx_swap(block, 1)
    diag = jnp.concatenate([ctx_swap(by_y[:half], 2), ctx_swap(by_x[half:], 4)])
    pair_x = ctx_swap(by_x, 1)
    pair_y = ctx_swap(by_y, 1)
    pair_diag = ctx_swap(diag, 1)
    return jnp.stack([block, own_pair, by_x, pair_x, by_y, pair_y, diag, pair_diag])


def ctx_scatter(blocks):
    if lax.axis_size("ctx") != 8:
        return lax.psum_scatter(blocks, "ctx", scatter_dimension=0, tiled=False).astype(F32)
    kept = blocks[0::2]
    pairs = kept + ctx_swap(blocks[1::2], 1)
    parts = [pairs[0]] + [ctx_swap(pairs[m], 2 * m) for m in (1, 2, 3)]
    return sum(part.astype(F32) for part in parts)


def depth_gather(block):
    size = lax.axis_size("fsdp")
    if size != 4:
        return lax.all_gather(block, "fsdp", axis=0)
    here = lax.axis_index("fsdp")
    out = jnp.zeros((size,) + block.shape, block.dtype)
    for step in range(size):
        part = block
        if step:
            part = lax.ppermute(block, "fsdp", [(at, (at + step) % size) for at in range(size)])
        out = lax.dynamic_update_index_in_dim(out, part, lax.rem(here - step + size, size), 0)
    return out


def depth_scatter(blocks):
    size = lax.axis_size("fsdp")
    if size != 4:
        return lax.psum_scatter(blocks, "fsdp", scatter_dimension=0, tiled=False).astype(F32)
    here = lax.axis_index("fsdp")
    total = lax.dynamic_index_in_dim(blocks, here, 0, False).astype(F32)
    for step in range(1, size):
        part = lax.dynamic_index_in_dim(blocks, lax.rem(here + step, size), 0, False)
        part = lax.ppermute(part, "fsdp", [(at, (at + step) % size) for at in range(size)])
        total = total + part.astype(F32)
    return total


def swap_place(base_ref, block):
    return jnp.bitwise_xor(base_ref[0], block)


def causal(rows, columns):
    keys = lax.broadcasted_iota(jnp.int32, (rows, columns), 0)
    queries = lax.broadcasted_iota(jnp.int32, (rows, columns), 1)
    return keys <= queries


def attend_kernel(
    blocks, tile, base_ref, qkv_ref, out_ref, out_t_ref, log_ref, q_ref, k_ref, v_t_ref
):
    length, width = out_ref.shape
    heads = width // HEAD_DIM
    rows = length // blocks
    for block in range(blocks):
        place = pl.multiple_of(swap_place(base_ref, block) * rows, rows)
        part = qkv_ref[block * rows : (block + 1) * rows, :]
        for head in range(heads):
            low, high = head * HEAD_DIM, (head + 1) * HEAD_DIM
            q_ref[head, pl.ds(place, rows), :] = part[:, low:high]
            k_ref[head, pl.ds(place, rows), :] = part[:, width + low : width + high]
        v_t_ref[:, pl.ds(place, rows)] = part[:, 2 * width :].T
    for q_tile in range(length // tile):
        columns = slice(q_tile * tile, (q_tile + 1) * tile)
        queries = [q_ref[head, columns, :] for head in range(heads)]

        def visit(k_tile, state, masked):
            start = pl.multiple_of(k_tile * tile, tile)
            result = []
            for head in range(heads):
                run_max, run_sum, run_acc = state[head]
                scores = times_trans(k_ref[head, pl.ds(start, tile), :], queries[head])
                if masked:
                    scores = jnp.where(causal(tile, tile), scores, MASKED)
                new_max = jnp.maximum(run_max, jnp.max(scores, 0, keepdims=True))
                weights = jnp.exp2(scores * EXP2_SCALE - new_max * EXP2_SCALE)
                factor = jnp.exp2((run_max - new_max) * EXP2_SCALE)
                new_sum = run_sum * factor + jnp.sum(weights, 0, keepdims=True)
                low, high = head * HEAD_DIM, (head + 1) * HEAD_DIM
                values = v_t_ref[low:high, pl.ds(start, tile)]
                new_acc = run_acc * factor + times(values, weights.astype(BF16))
                result.append((new_max, new_sum, new_acc))
            return result

        state = [
            (
                jnp.full((1, tile), MASKED, F32),
                jnp.zeros((1, tile), F32),
                jnp.zeros((HEAD_DIM, tile), F32),
            )
        ] * heads
        if q_tile:
            state = lax.fori_loop(0, q_tile, lambda at, st: visit(at, st, False), state)
        state = visit(q_tile, state, True)
        result = []
        for head in range(heads):
            run_max, run_sum, run_acc = state[head]
            result.append(run_acc / run_sum)
            log_ref[head : head + 1, columns] = run_max * EXP2_SCALE + jnp.log2(run_sum)
        result = jnp.concatenate(result, 0) if heads > 1 else result[0]
        out_t_ref[:, columns] = result
        out_ref[columns, :] = result.T.astype(BF16)


def attend_grad_kernel(
    blocks,
    tile,
    base_ref,
    qkv_ref,
    d_out_ref,
    out_t_ref,
    log_ref,
    d_qkv_ref,
    q_ref,
    k_ref,
    v_ref,
    k_t_ref,
    do_ref,
    delta_ref,
    dq_t_ref,
    dk_ref,
    dv_ref,
):
    length, width = d_out_ref.shape
    heads = width // HEAD_DIM
    rows = length // blocks
    for block in range(blocks):
        place = pl.multiple_of(swap_place(base_ref, block) * rows, rows)
        part = qkv_ref[block * rows : (block + 1) * rows, :]
        for head in range(heads):
            low, high = head * HEAD_DIM, (head + 1) * HEAD_DIM
            q_ref[head, pl.ds(place, rows), :] = part[:, low:high]
            k_ref[head, pl.ds(place, rows), :] = part[:, width + low : width + high]
            v_ref[head, pl.ds(place, rows), :] = part[:, 2 * width + low : 2 * width + high]
        k_t_ref[:, pl.ds(place, rows)] = part[:, width : 2 * width].T
        here = slice(block * rows, (block + 1) * rows)
        d_out = d_out_ref[here, :]
        product = d_out.astype(F32).T * out_t_ref[:, here]
        for head in range(heads):
            low, high = head * HEAD_DIM, (head + 1) * HEAD_DIM
            do_ref[head, here, :] = d_out[:, low:high]
            delta_ref[head : head + 1, here] = jnp.sum(product[low:high], 0, keepdims=True)
    dq_t_ref[...] = jnp.zeros_like(dq_t_ref)
    tiles = length // tile
    for k_tile in range(tiles):
        key_rows = slice(k_tile * tile, (k_tile + 1) * tile)

        def visit(q_tile, state, masked):
            start = pl.multiple_of(q_tile * tile, tile)
            query_rows = pl.ds(start, tile)
            result = []
            for head in range(heads):
                d_key, d_value = state[head]
                low, high = head * HEAD_DIM, (head + 1) * HEAD_DIM
                queries = q_ref[head, query_rows, :]
                d_out = do_ref[head, query_rows, :]
                scores = times_trans(k_ref[head, key_rows, :], queries)
                log_row = log_ref[head : head + 1, query_rows]
                probs = jnp.exp2(scores * EXP2_SCALE - log_row)
                if masked:
                    probs = jnp.where(causal(tile, tile), probs, 0.0)
                d_probs = times_trans(v_ref[head, key_rows, :], d_out)
                d_scores = (probs * (d_probs - delta_ref[head : head + 1, query_rows])).astype(BF16)
                d_value = d_value + times(probs.astype(BF16), d_out)
                d_key = d_key + times(d_scores, queries)
                dq_t_ref[low:high, query_rows] += times(k_t_ref[low:high, key_rows], d_scores)
                result.append((d_key, d_value))
            return result

        state = [(jnp.zeros((tile, HEAD_DIM), F32), jnp.zeros((tile, HEAD_DIM), F32))] * heads
        state = visit(k_tile, state, True)
        if k_tile + 1 < tiles:
            state = lax.fori_loop(k_tile + 1, tiles, lambda at, st: visit(at, st, False), state)
        for head in range(heads):
            dk_ref[head, key_rows, :] = state[head][0]
            dv_ref[head, key_rows, :] = state[head][1]
    for block in range(blocks):
        here = slice(block * rows, (block + 1) * rows)
        place = pl.ds(pl.multiple_of(swap_place(base_ref, block) * rows, rows), rows)
        d_key = [dk_ref[head, here, :] * SCORE_SCALE for head in range(heads)]
        d_value = [dv_ref[head, here, :] for head in range(heads)]
        parts = [dq_t_ref[:, here].T * SCORE_SCALE] + d_key + d_value
        d_qkv_ref[place, :] = jnp.concatenate(parts, 1).astype(BF16)


def attend(base, qkv, blocks):
    length, width = qkv.shape[0], qkv.shape[1] // 3
    heads = width // HEAD_DIM
    tile = min(512, length)
    return pl.pallas_call(
        functools.partial(attend_kernel, blocks, tile),
        out_shape=(
            jax.ShapeDtypeStruct((length, width), BF16),
            jax.ShapeDtypeStruct((width, length), F32),
            jax.ShapeDtypeStruct((heads, length), F32),
        ),
        in_specs=[
            pl.BlockSpec(memory_space=pltpu.SMEM),
            pl.BlockSpec(memory_space=pltpu.VMEM),
        ],
        out_specs=(pl.BlockSpec(memory_space=pltpu.VMEM),) * 3,
        scratch_shapes=[
            pltpu.VMEM((heads, length, HEAD_DIM), BF16),
            pltpu.VMEM((heads, length, HEAD_DIM), BF16),
            pltpu.VMEM((width, length), BF16),
        ],
        compiler_params=pltpu.CompilerParams(vmem_limit_bytes=40 << 20),
        cost_estimate=pl.CostEstimate(
            flops=2 * length * length * width,
            bytes_accessed=length * width * 12,
            transcendentals=heads * length * length // 2,
        ),
        name="attend",
    )(base, qkv)


def attend_grad(base, qkv, d_out, out_t, log_total, blocks):
    length, width = d_out.shape
    heads = width // HEAD_DIM
    tile = min(512, length)
    per_head = pltpu.VMEM((heads, length, HEAD_DIM), BF16)
    return pl.pallas_call(
        functools.partial(attend_grad_kernel, blocks, tile),
        out_shape=jax.ShapeDtypeStruct((length, 3 * width), BF16),
        in_specs=[pl.BlockSpec(memory_space=pltpu.SMEM)]
        + [pl.BlockSpec(memory_space=pltpu.VMEM)] * 4,
        out_specs=pl.BlockSpec(memory_space=pltpu.VMEM),
        scratch_shapes=[
            per_head,
            per_head,
            per_head,
            pltpu.VMEM((width, length), BF16),
            per_head,
            pltpu.VMEM((heads, length), F32),
            pltpu.VMEM((width, length), F32),
            pltpu.VMEM((heads, length, HEAD_DIM), F32),
            pltpu.VMEM((heads, length, HEAD_DIM), F32),
        ],
        compiler_params=pltpu.CompilerParams(vmem_limit_bytes=40 << 20),
        cost_estimate=pl.CostEstimate(
            flops=5 * length * length * width,
            bytes_accessed=length * width * 20,
            transcendentals=heads * length * length // 2,
        ),
        name="attend_grad",
    )(base, qkv, d_out, out_t, log_total)


def shards(
    block_in,
    out_grad,
    ln1_gain,
    ln1_shift,
    qkv_weight,
    query_bias,
    value_bias,
    proj_weight,
    proj_bias,
    ln2_gain,
    ln2_shift,
    up_weight,
    up_bias,
    down_weight,
    down_bias,
):
    seq_count, blk_len, model_dim = block_in.shape
    ctx_size, depth = lax.axis_size("ctx"), lax.axis_size("fsdp")
    ctx_index = lax.axis_index("ctx")
    base = ctx_base().reshape(1)
    seq_len = ctx_size * blk_len
    width = model_dim // ctx_size
    part = model_dim // depth
    hidden_part = up_bias.shape[0] // ctx_size
    hidden = hidden_part * depth

    own_in = block_in.reshape(blk_len, model_dim)
    own_dy = out_grad.reshape(blk_len, model_dim)

    def ctx_columns(value, columns, axis):
        return lax.dynamic_slice_in_dim(value, ctx_index * columns, columns, axis)

    qkv_slice = ctx_columns(qkv_weight.reshape(part, 3, model_dim), width, 2)
    vectors = [
        ln1_gain,
        ln1_shift,
        query_bias,
        value_bias,
        proj_bias,
        ln2_gain,
        ln2_shift,
        down_bias,
    ]
    first = jnp.concatenate(
        [qkv_slice.reshape(-1, 3 * width)]
        + [jnp.concatenate(vectors + [up_bias]).reshape(-1, 3 * width)]
    )
    first = depth_gather(first)
    qkv_full = first[:, :part].reshape(model_dim, 3 * width)
    vectors_full = first[:, part:].reshape(depth, -1).astype(F32)
    vectors_full, ubias_full = vectors_full[:, : 8 * part], vectors_full[:, 8 * part :]
    vectors_full = vectors_full.reshape(depth, 8, part).transpose(1, 0, 2).reshape(8, model_dim)
    gain_one, shift_one, qbias, vbias, pbias, gain_two, shift_two, dbias = vectors_full
    ubias = ctx_columns(ubias_full, hidden_part, 1).reshape(hidden)
    qkv_bias = jnp.concatenate(
        [ctx_columns(qbias, width, 0), jnp.zeros((width,), F32), ctx_columns(vbias, width, 0)]
    )

    all_in = ctx_gather(own_in).reshape(seq_len, model_dim)
    up_slice = lax.dynamic_index_in_dim(
        up_weight.reshape(part, depth, ctx_size, hidden_part), ctx_index, 2, False
    ).reshape(part, hidden)
    down_slice = ctx_columns(down_weight, hidden_part, 0)
    second = depth_gather(jnp.concatenate([up_slice, down_slice.reshape(-1, hidden)]))
    up_full = second[:, :part].reshape(model_dim, hidden)
    down_full = second[:, part:].reshape(hidden, model_dim)
    proj_rows = part // ctx_size
    proj_full = lax.all_gather(
        ctx_columns(proj_weight, proj_rows, 0), ("fsdp", "ctx"), axis=0, tiled=True
    )
    all_dy = ctx_gather(own_dy).reshape(seq_len, model_dim)

    normed = layer_norm(all_in.astype(F32), gain_one, shift_one).astype(BF16)
    qkv = (times(normed, qkv_full) + qkv_bias).astype(BF16)
    attn_heads, attn_trans, log_total = attend(base, qkv, ctx_size)
    attn_low = lax.all_to_all(
        attn_heads.reshape(ctx_size, blk_len, width), "ctx", 0, 0, tiled=False
    )
    attn_low = attn_low.transpose(1, 0, 2).reshape(blk_len, model_dim)

    own_f = own_in.astype(F32)
    resid_one = own_f + times(attn_low, proj_full) + pbias
    normed_two = layer_norm(resid_one, gain_two, shift_two).astype(BF16)

    all_two = ctx_gather(normed_two).reshape(seq_len, model_dim)
    pre_act = times(all_two, up_full) + ubias
    gelu_out, gelu_pull = jax.vjp(gelu_tanh, pre_act)
    hidden_low = gelu_out.astype(BF16)
    d_hidden = times_trans(all_dy, down_full)
    d_pre = gelu_pull(d_hidden)[0].astype(BF16)
    d_normed_two = times_trans(d_pre, up_full).astype(BF16)
    d_normed_two = ctx_scatter(d_normed_two.reshape(ctx_size, blk_len, model_dim))
    final_part = times(hidden_low, down_full).astype(BF16)
    final_sum = ctx_scatter(final_part.reshape(ctx_size, blk_len, model_dim))
    block_out = (resid_one + final_sum + dbias).astype(BF16).reshape(block_in.shape)
    d_up = contract_rows(all_two, d_pre).astype(BF16).reshape(depth, part, hidden)
    d_down = contract_rows(hidden_low, all_dy).astype(BF16).reshape(depth, hidden_part, model_dim)
    d_ubias = jnp.sum(d_pre.astype(F32), 0)

    norm_two_out, norm_two_pull = jax.vjp(layer_norm, resid_one, gain_two, shift_two)
    d_resid_part, d_gain_two, d_shift_two = norm_two_pull(d_normed_two)
    grad_f = own_dy.astype(F32)
    d_resid = grad_f + d_resid_part
    d_branch = d_resid.astype(BF16)
    d_attn = times_trans(d_branch, proj_full).astype(BF16)
    d_attn = d_attn.reshape(blk_len, ctx_size, width).transpose(1, 0, 2)
    d_attn = lax.all_to_all(d_attn, "ctx", 0, 0, tiled=False).reshape(seq_len, width)
    d_proj = contract_rows(attn_low, d_branch).astype(BF16)
    d_proj = d_proj.reshape(depth, ctx_size, proj_rows, model_dim)
    swapped = jnp.bitwise_xor(jnp.arange(ctx_size, dtype=jnp.int32), base)
    d_proj = jnp.take(d_proj, swapped, axis=1).transpose(1, 0, 2, 3)
    d_proj = ctx_scatter(d_proj).astype(BF16)

    d_qkv = attend_grad(base, qkv, d_attn, attn_trans, log_total, ctx_size)
    d_qkv_sum = jnp.sum(d_qkv.astype(F32), 0)
    d_normed = times_trans(d_qkv, qkv_full).astype(BF16)
    d_normed_own = ctx_scatter(d_normed.reshape(ctx_size, blk_len, model_dim))
    d_weight_qkv = contract_rows(normed, d_qkv).astype(BF16).reshape(depth, part, 3 * width)

    norm_all, norm_all_pull = jax.vjp(
        lambda gain, shift: layer_norm(all_in.astype(F32), gain, shift), gain_one, shift_one
    )
    d_gain_one, d_shift_one = norm_all_pull(d_normed.astype(F32))
    norm_one, norm_one_pull = jax.vjp(lambda value: layer_norm(value, gain_one, shift_one), own_f)
    d_input = (d_resid + norm_one_pull(d_normed_own)[0]).reshape(block_in.shape)

    def spread(value):
        return lax.all_gather(value.astype(BF16), "ctx", axis=0)

    d_up = spread(depth_scatter(d_up)).astype(F32)
    d_up = d_up.reshape(ctx_size, part, depth, hidden_part).transpose(1, 2, 0, 3)
    d_up = d_up.reshape(part, -1)
    d_down = spread(depth_scatter(d_down)).astype(F32).reshape(-1, model_dim)
    d_proj = spread(depth_scatter(d_proj)).astype(F32).reshape(part, model_dim)
    d_weight_qkv = spread(depth_scatter(d_weight_qkv)).astype(F32)
    d_weight_qkv = d_weight_qkv.reshape(ctx_size, part, 3, width).transpose(1, 2, 0, 3)
    d_weight_qkv = d_weight_qkv.reshape(part, -1)

    def widen(value, total):
        start = jnp.zeros(value.shape[:-1] + (total,), F32)
        return lax.dynamic_update_slice_in_dim(
            start, value, ctx_index * value.shape[-1], value.ndim - 1
        )

    small = [
        d_gain_one,
        d_shift_one,
        widen(d_qkv_sum[:width], model_dim),
        widen(d_qkv_sum[2 * width :], model_dim),
        jnp.sum(d_branch.astype(F32), 0),
        d_gain_two,
        d_shift_two,
        jnp.sum(grad_f, 0),
    ]
    small = jnp.stack(small).reshape(8, depth, part).transpose(1, 0, 2).reshape(depth, 8 * part)
    small = jnp.concatenate(
        [small, widen(d_ubias.reshape(depth, hidden_part), up_bias.shape[0])], 1
    )
    small = lax.psum(depth_scatter(small), "ctx")
    vec = small[: 8 * part].reshape(8, part)
    return (
        block_out,
        d_input,
        vec[0],
        vec[1],
        d_weight_qkv,
        vec[2],
        vec[3],
        d_proj,
        vec[4],
        vec[5],
        vec[6],
        d_up,
        small[8 * part :],
        d_down,
        vec[7],
    )


def solution(mesh):
    rows, matrix, vector = P("fsdp", "ctx", None), P("fsdp", None), P("fsdp")
    in_specs = (
        rows,
        rows,
        vector,
        vector,
        matrix,
        vector,
        vector,
        matrix,
        vector,
        vector,
        vector,
        matrix,
        vector,
        matrix,
        vector,
    )
    out_specs = (rows, rows) + in_specs[2:]
    return jax.shard_map(shards, mesh=mesh, in_specs=in_specs, out_specs=out_specs, check_vma=False)
```

time: 1340 us -> 532 us (0.40)
  waiting for transfers between devices: 965 us -> 162 us
  starting transfers between devices: 0.73 us -> 86.5 us
  blocking collectives: 117 us -> 33.5 us
  matrix products: 123 us -> 43.6 us
  local copies, waits for them, and re-layouts: 71.3 us -> 111 us
  Pallas kernels: 0 us -> 28.8 us
    reduce_scatter x6 -> x0, waiting for transfers between devices: 532 us -> none  [the longest x1 148 us: shards(): lax.psum_scatter(d_up.astype(jnp.bfloat16), 'fsdp', scatter_dimension=0,...]
    all_gather x6 -> x4, waiting for transfers between devices: 384 us -> 0.01 us  [the longest x3 0.01 us: spread(): return lax.all_gather(value.astype(BF16), 'ctx', axis=0)]
    ppermute x0 -> x61, waiting for transfers between devices: none -> 155 us  [the longest x40 64.4 us: ctx_swap(): return lax.ppermute(value, 'ctx', [(at, at ^ bits) for at in range(size)])]
    ppermute x0 -> x61, starting transfers between devices: none -> 78.6 us  [the longest x40 33.9 us: ctx_swap(): return lax.ppermute(value, 'ctx', [(at, at ^ bits) for at in range(size)])]
    all_gather x9 -> x1, blocking collectives: 88 us -> 10.4 us  [spread(): return lax.all_gather(value.astype(BF16), 'ctx', axis=0)]
    dot_general x60 -> x4, matrix products: 78.6 us -> 10.3 us  [times(): return jnp.dot(left, right, preferred_element_type=F32)]
    psum x1 -> x0, waiting for transfers between devices: 46.3 us -> none  [shards(): lax.psum(summed[2].astype(jnp.bfloat16), 'ctx').astype(jnp.float32)]
    unnamed x62 -> x104, local copies, waits for them, and re-layouts: 18.6 us -> 50.6 us
  transfers between devices with their start and end apart: 13 -> 67, of which waited for: 11 -> 21; matrix products, arithmetic and copies ran while one was open for 9% -> 30% of each run, Pallas kernels for 0% -> 6%
where the time goes in v1:
time: 532 us; the launch traced here: 524 us
  waiting for transfers between devices  162 us (30%)
  local copies, waits for them, and re-layouts  111 us (21%)
  starting transfers between devices  86.5 us (16%)
  matrix products  43.6 us (8%)
  other arithmetic  42.8 us (8%)
  blocking collectives  33.5 us (6%)
  Pallas kernels  28.8 us (5%)
  between operations  15.2 us (3%)
    ppermute x40, waiting for transfers between devices, ctx_swap(): return lax.ppermute(value, 'ctx', [(at, at ^ bits) for at in range(size)])  64.4 us
    unnamed x104, local copies, waits for them, and re-layouts  50.6 us
    ppermute x15, waiting for transfers between devices, depth_scatter(): lax.ppermute(part, 'fsdp', [(at, (at + step) % size) for at in range(size)])  46.4 us
    ppermute x6, waiting for transfers between devices, depth_gather(): lax.ppermute(block, 'fsdp', [(at, (at + step) % size) for at in range(siz...  44.5 us
    ppermute x40, starting transfers between devices, ctx_swap(): return lax.ppermute(value, 'ctx', [(at, at ^ bits) for at in range(size)])  33.9 us
    ppermute x15, starting transfers between devices, depth_scatter(): lax.ppermute(part, 'fsdp', [(at, (at + step) % size) for at in range(size)])  30.9 us
    psum x1, blocking collectives, shards(): small = lax.psum(depth_scatter(small), 'ctx')  23.1 us
    dot_general x4, matrix products, times_trans(): lax.dot_general(left, right, (((1,), (1,)), ((), ())), preferred_element_...  21.9 us
  transfers between devices with their start and end apart: 67, of which 21 were waited for; matrix products, arithmetic and copies ran while one was open for 30% of the time, Pallas kernels for 6%

profile of v1, /device:TPU:0, one launch (start us, length us, event | category | flops | bytes accessed | tf_op | source)
XLA Modules:
  0.0 524.2 jit_solution(12899813176618405706)
XLA Ops:
  18.5 4.1 collective-permute-start.9
  26.7 4.1 copy.48
  37.2 6.9 %collective-permute-done.9 = bf16[264,384]{0,1:T(8,128)(2,1)} collective-permute-done((bf16[264,384]{0,1:T(8,128)(2,1)S(1)}, bf16[264,384]{0,1:T(8,128)(2,1)}, u32[]{:S(2)}, u32[]{:S(2)}) %collective-permute-start.9) | collective-permute-done | bytes 202784 | tf_op jit(solution)/shard_map/ppermute | solution.py:88
  50.1 5.3 %collective-permute-start.21 = (bf16[512,512]{0,1:T(8,128)(2,1)}, bf16[512,512]{0,1:T(8,128)(2,1)}, u32[]{:S(2)}, u32[]{:S(2)}) collective-permute-start(bf16[512,512]{0,1:T(8,128)(2,1)} %get-tuple-element.81), channel_id=1, source_target_pairs={{0,3},{1,0},{2,1},{3,2},{4,7},{5,4},{6,5},{7,6},{8,11},{9,8},{10,9... | collective-permute-start | bytes 1572872 | tf_op jit(solution)/shard_map/ppermute | solution.py:88
  56.7 29.8 %collective-permute-done.20 = bf16[512,512]{0,1:T(8,128)(2,1)} collective-permute-done((bf16[512,512]{0,1:T(8,128)(2,1)}, bf16[512,512]{0,1:T(8,128)(2,1)}, u32[]{:S(2)}, u32[]{:S(2)}) %collective-permute-start.20) | collective-permute-done | bytes 524320 | tf_op jit(solution)/shard_map/ppermute | solution.py:88
  90.1 7.8 %collective-permute-done.21 = bf16[512,512]{0,1:T(8,128)(2,1)} collective-permute-done((bf16[512,512]{0,1:T(8,128)(2,1)}, bf16[512,512]{0,1:T(8,128)(2,1)}, u32[]{:S(2)}, u32[]{:S(2)}) %collective-permute-start.21) | collective-permute-done | bytes 524320 | tf_op jit(solution)/shard_map/ppermute | solution.py:88
  136.3 2.8 convert_reduce_fusion.1
  139.1 3.0 multiply_reduce_fusion
  142.2 3.4 add_convert_fusion.1
  148.0 12.4 %attend.1 = (bf16[2048,128]{1,0:T(8,128)(2,1)S(1)}, f32[128,2048]{1,0:T(8,128)S(1)}, f32[2,2048]{1,0:T(2,128)S(1)}) custom-call(s32[1]{0:T(128)} %bitcast.1.base_ref, bf16[2048,384]{1,0:T(8,128)(2,1)S(1)} %add_convert_fusion.2.qkv_ref), custom_call_target="tpu_custom_call" | custom-call | flops 1073741824 | bytes 3145728 | tf_op jit(solution)/shard_map/attend/pallas_call | solution.py:257
  162.6 3.6 all-to-all-start
  168.9 7.0 %all-to-all-done = bf16[8,256,128]{1,2,0:T(8,128)(2,1)S(1)} async-done(((bf16[8,256,128]{1,2,0:T(8,128)(2,1)}), bf16[8,256,128]{1,2,0:T(8,128)(2,1)S(1)}, u32[]{:S(2)}, u32[]{:S(2)}) %all-to-all-start) | async-done | bytes 524320 | tf_op jit(solution)/shard_map/all_to_all | solution.py:392
  185.8 6.0 %collective-permute-done.12 = bf16[256,1024]{1,0:T(8,128)(2,1)S(1)} collective-permute-done((bf16[256,1024]{1,0:T(8,128)(2,1)S(1)}, bf16[256,1024]{1,0:T(8,128)(2,1)S(1)}, u32[]{:S(2)}, u32[]{:S(2)}) %collective-permute-start.12) | collective-permute-done | bytes 524320 | tf_op jit(solution)/shard_map/ppermute | solution.py:49
  196.2 5.9 %collective-permute-done.16 = bf16[128,1024]{1,0:T(8,128)(2,1)S(1)} collective-permute-done((bf16[128,1024]{1,0:T(8,128)(2,1)S(1)}, bf16[128,1024]{1,0:T(8,128)(2,1)S(1)}, u32[]{:S(2)}, u32[]{:S(2)}) %collective-permute-start.16) | collective-permute-done | bytes 262176 | tf_op jit(solution)/shard_map/ppermute | solution.py:49
  206.5 9.5 %convert_reduce_fusion.2 = (f32[512]{0:T(512)S(1)}, bf16[2048,512]{1,0:T(8,128)(2,1)S(1)}) fusion(f32[2048,512]{1,0:T(8,128)S(1)} %fusion.63, f32[512]{0:T(512)S(1)} %fusion.46, bf16[2048,1024]{1,0:T(8,128)(2,1)} %bitcast.60, bf16[512,1024]{1,0:T(8,128)(2,1)S(1)} %copy-done.20), kind=kOutput, calls=%fused_computation.21 | convolution fusion | flops 2175794688 | bytes 11538432 | tf_op jit(solution)/shard_map/dot_general | solution.py:40
  220.2 6.8 %collective-permute-start.55 = (bf16[256,512]{1,0:T(8,128)(2,1)}, bf16[256,512]{1,0:T(8,128)(2,1)S(1)}, u32[]{:S(2)}, u32[]{:S(2)}) collective-permute-start(bf16[256,512]{1,0:T(8,128)(2,1)} %get-tuple-element.69), channel_id=1, source_target_pairs={{0,1},{1,2},{2,3},{3,0},{4,5},{5,6},{6,7},{7,4},{8,9},{9,10},{10,1... | collective-permute-start | bytes 786440 | tf_op jit(solution)/shard_map/ppermute | solution.py:101
  227.0 2.9 collective-permute-start.56
  229.9 4.1 collective-permute-done.55
  234.0 5.7 %collective-permute-done.57 = bf16[256,512]{1,0:T(8,128)(2,1)S(1)} collective-permute-done((bf16[256,512]{1,0:T(8,128)(2,1)}, bf16[256,512]{1,0:T(8,128)(2,1)S(1)}, u32[]{:S(2)}, u32[]{:S(2)}) %collective-permute-start.57) | collective-permute-done | bytes 262176 | tf_op jit(solution)/shard_map/ppermute | solution.py:101
  239.7 8.0 %collective-permute-done.56 = bf16[256,512]{1,0:T(8,128)(2,1)} collective-permute-done((bf16[256,512]{1,0:T(8,128)(2,1)S(1)}, bf16[256,512]{1,0:T(8,128)(2,1)}, u32[]{:S(2)}, u32[]{:S(2)}) %collective-permute-start.56) | collective-permute-done | bytes 262176 | tf_op jit(solution)/shard_map/ppermute | solution.py:101
  250.0 4.4 convolution_convert_fusion.1
  257.1 2.9 convolution_convert_fusion.2
  262.1 4.7 convolution_convert_fusion.4
  266.9 3.7 collective-permute-start.58
  270.7 3.0 collective-permute-start.60
  274.2 6.6 %collective-permute-done.58 = bf16[128,1024]{1,0:T(8,128)(2,1)S(1)} collective-permute-done((bf16[128,1024]{1,0:T(8,128)(2,1)S(1)}, bf16[128,1024]{1,0:T(8,128)(2,1)S(1)}, u32[]{:S(2)}, u32[]{:S(2)}) %collective-permute-start.58) | collective-permute-done | bytes 262176 | tf_op jit(solution)/shard_map/ppermute | solution.py:101
  280.8 3.9 collective-permute-done.60
  284.7 12.7 %collective-permute-done.59 = bf16[128,1024]{1,0:T(8,128)(2,1)S(1)} collective-permute-done((bf16[128,1024]{1,0:T(8,128)(2,1)S(1)}, bf16[128,1024]{1,0:T(8,128)(2,1)S(1)}, u32[]{:S(2)}, u32[]{:S(2)}) %collective-permute-start.59) | collective-permute-done | bytes 262176 | tf_op jit(solution)/shard_map/ppermute | solution.py:101
  308.7 10.0 %collective-permute-done.35 = bf16[256,1024]{1,0:T(8,128)(2,1)S(1)} collective-permute-done((bf16[256,1024]{1,0:T(8,128)(2,1)S(1)}, bf16[256,1024]{1,0:T(8,128)(2,1)S(1)}, u32[]{:S(2)}, u32[]{:S(2)}) %collective-permute-start.35) | collective-permute-done | bytes 524320 | tf_op jit(solution)/shard_map/ppermute | solution.py:49
  319.2 16.3 %collective-permute-done.37 = bf16[256,1024]{1,0:T(8,128)(2,1)S(1)} collective-permute-done((bf16[256,1024]{1,0:T(8,128)(2,1)S(1)}, bf16[256,1024]{1,0:T(8,128)(2,1)S(1)}, u32[]{:S(2)}, u32[]{:S(2)}) %collective-permute-start.37) | collective-permute-done | bytes 524320 | tf_op jit(solution)/shard_map/ppermute | solution.py:49
  336.3 10.5 %collective-permute-done.23 = bf16[256,1024]{1,0:T(8,128)(2,1)S(1)} collective-permute-done((bf16[256,1024]{1,0:T(8,128)(2,1)S(1)}, bf16[256,1024]{1,0:T(8,128)(2,1)S(1)}, u32[]{:S(2)}, u32[]{:S(2)}) %collective-permute-start.23) | collective-permute-done | bytes 524320 | tf_op jit(solution)/shard_map/ppermute | solution.py:49
  346.8 10.5 %collective-permute-done.25 = bf16[256,1024]{1,0:T(8,128)(2,1)S(1)} collective-permute-done((bf16[256,1024]{1,0:T(8,128)(2,1)S(1)}, bf16[256,1024]{1,0:T(8,128)(2,1)S(1)}, u32[]{:S(2)}, u32[]{:S(2)}) %collective-permute-start.25) | collective-permute-done | bytes 524320 | tf_op jit(solution)/shard_map/ppermute | solution.py:49
  362.0 3.5 all-to-all-start.1
  368.0 3.6 gather_fusion
  377.0 16.5 %attend_grad.1 = bf16[2048,384]{1,0:T(8,128)(2,1)S(1)} custom-call(s32[1]{0:T(128)} %bitcast.1.base_ref, bf16[2048,384]{1,0:T(8,128)(2,1)S(1)} %copy-done.3, bf16[2048,128]{1,0:T(8,128)(2,1)S(1)} %bitcast.268, f32[128,2048]{1,0:T(8,128)S(1)} %get-tuple-element.19.out_t_ref, f32[2,2048]{1,0:T(2,128)S(1)} %get-tuple-element.20.log_ref), custom_call_target="tpu_custom_call" | custom-call | flops 2684354560 | bytes 5242880 | tf_op jit(solution)/shard_map/attend_grad/pallas_call | solution.py:289
  395.7 7.2 %convert_reduce_fusion = (f32[1024]{0:T(1024)S(1)}, f32[1024]{0:T(1024)S(1)}, bf16[2048,1024]{1,0:T(8,128)(2,1)}, bf16[2048,1024]{1,0:T(8,128)(2,1)}) fusion(f32[2048]{0:T(1024)S(1)} %bitcast.331, f32[2048]{0:T(1024)S(1)} %bitcast.330, bf16[8,256,1024]{2,1,0:T(8,128)(2,1)} %bitcast_dynamic-update-slice_fusion.15, f32[1024]{0:T(1024)S(1)} %bitcast.324, ...), kind=kOutput, calls=%fused_computation.1 | convolution fusion | flops 1633679360 | bytes 14974976 | tf_op jit(solution)/shard_map/dot_general | solution.py:40
  403.0 3.2 slice.191
  409.3 3.8 collective-permute-start.44
  417.4 3.0 collective-permute-start.47
  423.3 2.8 collective-permute-start.51
  426.1 4.4 collective-permute-done.46
  432.1 23.1 %psum.7 = f32[3072]{0:T(1024)S(1)} all-reduce(f32[3072]{0:T(1024)S(1)} %add_add_fusion.2), channel_id=1, replica_groups=mesh['ctx'=8,'fsdp'=4] {'ctx'}, use_global_device_ids=true, to_apply=%region_18.19 | all-reduce | flops 3072 | bytes 24576 | tf_op jit(solution)/shard_map/psum | solution.py:475
  471.2 4.7 reshape.500
  475.9 4.8 copy.60
  480.7 5.8 %copy.73 = f32[32,8,32,128]{3,1,2,0:T(8,128)} copy(f32[32,8,32,128]{3,2,1,0:T(8,128)S(1)} %bitcast.270) | data formatting | bytes 8388608
  486.5 4.1 reshape.515
  491.6 10.4 %all-gather.1 = bf16[256,1024]{1,0:T(8,128)(2,1)S(1)} all-gather(bf16[32,1024]{1,0:T(8,128)(2,1)S(1)} %fusion.41), channel_id=3, replica_groups=mesh['ctx'=8,'fsdp'=4] {'ctx'}, dimensions={0}, use_global_device_ids=true | all-gather | bytes 589824 | tf_op jit(solution)/shard_map/all_gather | solution.py:444
  513.9 3.5 copy.61
  (345 shorter events, 176.4 us)
Async XLA Ops:
  7.2 168.7 %all-gather.9.cloned.1.call-start = ((), (), s32[]{:S(2)}) async-start(), calls=%async_computation.2 | async-start | bytes 2162688 | tf_op jit(solution)/shard_map/all_gather | solution.py:384
  18.5 25.6 %collective-permute-start.9 = (bf16[264,384]{0,1:T(8,128)(2,1)S(1)}, bf16[264,384]{0,1:T(8,128)(2,1)}, u32[]{:S(2)}, u32[]{:S(2)}) collective-permute-start(bf16[264,384]{0,1:T(8,128)(2,1)S(1)} %get-tuple-element.83), channel_id=1, source_target_pairs={{0,2},{1,3},{2,0},{3,1},{4,6},{5,7},{6,4},{7,5},{8,10},{9,11},{10,... | collective-permute-start | bytes 608264 | tf_op jit(solution)/shard_map/ppermute | solution.py:88
  22.6 24.7 %collective-permute-start.8 = (bf16[264,384]{0,1:T(8,128)(2,1)S(1)}, bf16[264,384]{0,1:T(8,128)(2,1)}, u32[]{:S(2)}, u32[]{:S(2)}) collective-permute-start(bf16[264,384]{0,1:T(8,128)(2,1)S(1)} %get-tuple-element.83), channel_id=1, source_target_pairs={{0,1},{1,2},{2,3},{3,0},{4,5},{5,6},{6,7},{7,4},{8,9},{9,10},{10,1... | collective-permute-start | bytes 608264 | tf_op jit(solution)/shard_map/ppermute | solution.py:88
  24.2 25.9 %collective-permute-start.10 = (bf16[264,384]{0,1:T(8,128)(2,1)S(1)}, bf16[264,384]{0,1:T(8,128)(2,1)}, u32[]{:S(2)}, u32[]{:S(2)}) collective-permute-start(bf16[264,384]{0,1:T(8,128)(2,1)S(1)} %get-tuple-element.83), channel_id=1, source_target_pairs={{0,3},{1,0},{2,1},{3,2},{4,7},{5,4},{6,5},{7,6},{8,11},{9,8},{10,9... | collective-permute-start | bytes 608264 | tf_op jit(solution)/shard_map/ppermute | solution.py:88
  32.7 53.8 %collective-permute-start.20 = (bf16[512,512]{0,1:T(8,128)(2,1)}, bf16[512,512]{0,1:T(8,128)(2,1)}, u32[]{:S(2)}, u32[]{:S(2)}) collective-permute-start(bf16[512,512]{0,1:T(8,128)(2,1)} %get-tuple-element.81), channel_id=1, source_target_pairs={{0,2},{1,3},{2,0},{3,1},{4,6},{5,7},{6,4},{7,5},{8,10},{9,11},{10,... | collective-permute-start | bytes 1572872 | tf_op jit(solution)/shard_map/ppermute | solution.py:88
  32.7 55.8 %collective-permute-start.19 = (bf16[512,512]{0,1:T(8,128)(2,1)}, bf16[512,512]{0,1:T(8,128)(2,1)}, u32[]{:S(2)}, u32[]{:S(2)}) collective-permute-start(bf16[512,512]{0,1:T(8,128)(2,1)} %get-tuple-element.81), channel_id=1, source_target_pairs={{0,1},{1,2},{2,3},{3,0},{4,5},{5,6},{6,7},{7,4},{8,9},{9,10},{10,1... | collective-permute-start | bytes 1572872 | tf_op jit(solution)/shard_map/ppermute | solution.py:88
  44.1 58.7 %collective-permute-start.1 = (bf16[256,1024]{1,0:T(8,128)(2,1)S(1)}, bf16[256,1024]{1,0:T(8,128)(2,1)}, u32[]{:S(2)}, u32[]{:S(2)}) collective-permute-start(bf16[256,1024]{1,0:T(8,128)(2,1)S(1)} %bitcast.271), channel_id=1, source_target_pairs={{0,8},{4,12},{8,0},{12,4},{16,24},{20,28},{24,16},{28,20},{1,9},{5... | collective-permute-start | bytes 1572872 | tf_op jit(solution)/shard_map/ppermute | solution.py:49
  47.4 57.7 %collective-permute-start.3 = (bf16[256,1024]{1,0:T(8,128)(2,1)S(1)}, bf16[256,1024]{1,0:T(8,128)(2,1)S(1)}, u32[]{:S(2)}, u32[]{:S(2)}) collective-permute-start(bf16[256,1024]{1,0:T(8,128)(2,1)S(1)} %bitcast.272), channel_id=1, source_target_pairs={{0,16},{4,20},{8,24},{12,28},{16,0},{20,4},{24,8},{28,12},{1,17},{... | collective-permute-start | bytes 1572872 | tf_op jit(solution)/shard_map/ppermute | solution.py:49
  50.1 47.8 %collective-permute-start.21 = (bf16[512,512]{0,1:T(8,128)(2,1)}, bf16[512,512]{0,1:T(8,128)(2,1)}, u32[]{:S(2)}, u32[]{:S(2)}) collective-permute-start(bf16[512,512]{0,1:T(8,128)(2,1)} %get-tuple-element.81), channel_id=1, source_target_pairs={{0,3},{1,0},{2,1},{3,2},{4,7},{5,4},{6,5},{7,6},{8,11},{9,8},{10,9... | collective-permute-start | bytes 1572872 | tf_op jit(solution)/shard_map/ppermute | solution.py:88
  86.4 20.7 %collective-permute-start.27 = (bf16[256,1024]{1,0:T(8,128)(2,1)S(1)}, bf16[256,1024]{1,0:T(8,128)(2,1)}, u32[]{:S(2)}, u32[]{:S(2)}) collective-permute-start(bf16[256,1024]{1,0:T(8,128)(2,1)S(1)} %bitcast.278), channel_id=1, source_target_pairs={{0,8},{4,12},{8,0},{12,4},{16,24},{20,28},{24,16},{28,20},{1,9},{5... | collective-permute-start | bytes 1572872 | tf_op jit(solution)/shard_map/ppermute | solution.py:49
  88.5 21.8 %collective-permute-start.29 = (bf16[256,1024]{1,0:T(8,128)(2,1)S(1)}, bf16[256,1024]{1,0:T(8,128)(2,1)}, u32[]{:S(2)}, u32[]{:S(2)}) collective-permute-start(bf16[256,1024]{1,0:T(8,128)(2,1)S(1)} %bitcast.279), channel_id=1, source_target_pairs={{0,16},{4,20},{8,24},{12,28},{16,0},{20,4},{24,8},{28,12},{1,17},{... | collective-permute-start | bytes 1572872 | tf_op jit(solution)/shard_map/ppermute | solution.py:49
  97.9 17.1 %collective-permute-start.26 = (bf16[256,1024]{1,0:T(8,128)(2,1)S(1)}, bf16[256,1024]{1,0:T(8,128)(2,1)}, u32[]{:S(2)}, u32[]{:S(2)}) collective-permute-start(bf16[256,1024]{1,0:T(8,128)(2,1)S(1)} %bitcast.280), channel_id=1, source_target_pairs={{0,4},{4,0},{8,12},{12,8},{16,20},{20,16},{24,28},{28,24},{1,5},{5... | collective-permute-start | bytes 1572872 | tf_op jit(solution)/shard_map/ppermute | solution.py:49
  102.8 19.2 %collective-permute-start = (bf16[256,1024]{1,0:T(8,128)(2,1)S(1)}, bf16[256,1024]{1,0:T(8,128)(2,1)S(1)}, u32[]{:S(2)}, u32[]{:S(2)}) collective-permute-start(bf16[256,1024]{1,0:T(8,128)(2,1)S(1)} %bitcast.273), channel_id=1, source_target_pairs={{0,4},{4,0},{8,12},{12,8},{16,20},{20,16},{24,28},{28,24},{1,5},{5... | collective-permute-start | bytes 1572872 | tf_op jit(solution)/shard_map/ppermute | solution.py:49
  105.1 24.3 %collective-permute-start.6 = (bf16[128,1024]{1,0:T(8,128)(2,1)}, bf16[128,1024]{1,0:T(8,128)(2,1)S(1)}, u32[]{:S(2)}, u32[]{:S(2)}) collective-permute-start(bf16[128,1024]{1,0:T(8,128)(2,1)} %slice.216), channel_id=1, source_target_pairs={{0,16},{4,20},{8,24},{12,28},{16,0},{20,4},{24,8},{28,12},{1,17},{... | collective-permute-start | bytes 786440 | tf_op jit(solution)/shard_map/ppermute | solution.py:49
  107.1 19.0 %collective-permute-start.5 = (bf16[128,1024]{1,0:T(8,128)(2,1)}, bf16[128,1024]{1,0:T(8,128)(2,1)}, u32[]{:S(2)}, u32[]{:S(2)}) collective-permute-start(bf16[128,1024]{1,0:T(8,128)(2,1)} %slice.215), channel_id=1, source_target_pairs={{0,8},{4,12},{8,0},{12,4},{16,24},{20,28},{24,16},{28,20},{1,9},{5... | collective-permute-start | bytes 786440 | tf_op jit(solution)/shard_map/ppermute | solution.py:49
  110.3 19.6 %collective-permute-start.32 = (bf16[128,1024]{1,0:T(8,128)(2,1)}, bf16[128,1024]{1,0:T(8,128)(2,1)}, u32[]{:S(2)}, u32[]{:S(2)}) collective-permute-start(bf16[128,1024]{1,0:T(8,128)(2,1)} %slice.230), channel_id=1, source_target_pairs={{0,16},{4,20},{8,24},{12,28},{16,0},{20,4},{24,8},{28,12},{1,17},{... | collective-permute-start | bytes 786440 | tf_op jit(solution)/shard_map/ppermute | solution.py:49
  127.6 38.5 %collective-permute-start.28 = (bf16[256,1024]{1,0:T(8,128)(2,1)}, bf16[256,1024]{1,0:T(8,128)(2,1)S(1)}, u32[]{:S(2)}, u32[]{:S(2)}) collective-permute-start(bf16[256,1024]{1,0:T(8,128)(2,1)} %collective-permute-done.27), channel_id=1, source_target_pairs={{0,4},{4,0},{8,12},{12,8},{16,20},{20,16},{24,28},{28,24},{1,5},{5... | collective-permute-start | bytes 1572872 | tf_op jit(solution)/shard_map/ppermute | solution.py:49
  129.4 50.8 %collective-permute-start.30 = (bf16[256,1024]{1,0:T(8,128)(2,1)}, bf16[256,1024]{1,0:T(8,128)(2,1)}, u32[]{:S(2)}, u32[]{:S(2)}) collective-permute-start(bf16[256,1024]{1,0:T(8,128)(2,1)} %collective-permute-done.29), channel_id=1, source_target_pairs={{0,4},{4,0},{8,12},{12,8},{16,20},{20,16},{24,28},{28,24},{1,5},{5... | collective-permute-start | bytes 1572872 | tf_op jit(solution)/shard_map/ppermute | solution.py:49
  131.7 52.3 %collective-permute-start.33 = (bf16[256,1024]{1,0:T(8,128)(2,1)}, bf16[256,1024]{1,0:T(8,128)(2,1)}, u32[]{:S(2)}, u32[]{:S(2)}) collective-permute-start(bf16[256,1024]{1,0:T(8,128)(2,1)} %constant_dynamic-update-slice_fusion.5), channel_id=1, source_target_pairs={{0,4},{4,0},{8,12},{12,8},{16,20},{20,16},{24,28},{28,24},{1,5},{5... | collective-permute-start | bytes 1572872 | tf_op jit(solution)/shard_map/ppermute | solution.py:49
  166.1 305.1 %all-gather.13.cloned.1.call-start = ((), (), s32[]{:S(2)}) async-start(), calls=%async_computation.4 | async-start | bytes 2359296 | tf_op jit(solution)/shard_map/all_gather | solution.py:444
  179.7 16.4 %collective-permute-start.11 = (bf16[256,1024]{1,0:T(8,128)(2,1)S(1)}, bf16[256,1024]{1,0:T(8,128)(2,1)S(1)}, u32[]{:S(2)}, u32[]{:S(2)}) collective-permute-start(bf16[256,1024]{1,0:T(8,128)(2,1)S(1)} %get-tuple-element.53), channel_id=1, source_target_pairs={{0,4},{4,0},{8,12},{12,8},{16,20},{20,16},{24,28},{28,24},{1,5},{5... | collective-permute-start | bytes 1572872 | tf_op jit(solution)/shard_map/ppermute | solution.py:49
  179.7 14.7 %collective-permute-start.14 = (bf16[256,1024]{1,0:T(8,128)(2,1)S(1)}, bf16[256,1024]{1,0:T(8,128)(2,1)S(1)}, u32[]{:S(2)}, u32[]{:S(2)}) collective-permute-start(bf16[256,1024]{1,0:T(8,128)(2,1)S(1)} %get-tuple-element.53), channel_id=1, source_target_pairs={{0,16},{4,20},{8,24},{12,28},{16,0},{20,4},{24,8},{28,12},{1,17},{... | collective-permute-start | bytes 1572872 | tf_op jit(solution)/shard_map/ppermute | solution.py:49
  227.0 20.6 %collective-permute-start.56 = (bf16[256,512]{1,0:T(8,128)(2,1)S(1)}, bf16[256,512]{1,0:T(8,128)(2,1)}, u32[]{:S(2)}, u32[]{:S(2)}) collective-permute-start(bf16[256,512]{1,0:T(8,128)(2,1)S(1)} %get-tuple-element.71), channel_id=1, source_target_pairs={{0,2},{1,3},{2,0},{3,1},{4,6},{5,7},{6,4},{7,5},{8,10},{9,11},{10,... | collective-permute-start | bytes 786440 | tf_op jit(solution)/shard_map/ppermute | solution.py:101
  249.6 236.9 %all-gather.15.cloned.1.call-start = ((), (), s32[]{:S(2)}) async-start(), calls=%async_computation.5 | async-start | bytes 2359296 | tf_op jit(solution)/shard_map/all_gather | solution.py:444
  257.0 41.3 %collective-permute-start.34 = (bf16[4,256,1024]{2,1,0:T(8,128)(2,1)}, bf16[4,256,1024]{2,1,0:T(8,128)(2,1)}, u32[]{:S(2)}, u32[]{:S(2)}) collective-permute-start(bf16[4,256,1024]{2,1,0:T(8,128)(2,1)} %slice.185), channel_id=1, source_target_pairs={{0,4},{4,0},{8,12},{12,8},{16,20},{20,16},{24,28},{28,24},{1,5},{5... | collective-permute-start | bytes 6291464 | tf_op jit(solution)/shard_map/ppermute | solution.py:49
  261.6 43.0 %collective-permute-start.22 = (bf16[4,256,1024]{2,1,0:T(8,128)(2,1)}, bf16[4,256,1024]{2,1,0:T(8,128)(2,1)}, u32[]{:S(2)}, u32[]{:S(2)}) collective-permute-start(bf16[4,256,1024]{2,1,0:T(8,128)(2,1)} %slice.177), channel_id=1, source_target_pairs={{0,4},{4,0},{8,12},{12,8},{16,20},{20,16},{24,28},{28,24},{1,5},{5... | collective-permute-start | bytes 6291464 | tf_op jit(solution)/shard_map/ppermute | solution.py:49
  266.9 13.9 %collective-permute-start.58 = (bf16[128,1024]{1,0:T(8,128)(2,1)S(1)}, bf16[128,1024]{1,0:T(8,128)(2,1)S(1)}, u32[]{:S(2)}, u32[]{:S(2)}) collective-permute-start(bf16[128,1024]{1,0:T(8,128)(2,1)S(1)} %get-tuple-element.66), channel_id=1, source_target_pairs={{0,1},{1,2},{2,3},{3,0},{4,5},{5,6},{6,7},{7,4},{8,9},{9,10},{10,1... | collective-permute-start | bytes 786440 | tf_op jit(solution)/shard_map/ppermute | solution.py:101
  270.7 14.0 %collective-permute-start.60 = (bf16[128,1024]{1,0:T(8,128)(2,1)S(1)}, bf16[128,1024]{1,0:T(8,128)(2,1)S(1)}, u32[]{:S(2)}, u32[]{:S(2)}) collective-permute-start(bf16[128,1024]{1,0:T(8,128)(2,1)S(1)} %get-tuple-element.67), channel_id=1, source_target_pairs={{0,3},{1,0},{2,1},{3,2},{4,7},{5,4},{6,5},{7,6},{8,11},{9,8},{10,9... | collective-permute-start | bytes 786440 | tf_op jit(solution)/shard_map/ppermute | solution.py:101
  273.7 23.7 %collective-permute-start.59 = (bf16[128,1024]{1,0:T(8,128)(2,1)S(1)}, bf16[128,1024]{1,0:T(8,128)(2,1)S(1)}, u32[]{:S(2)}, u32[]{:S(2)}) collective-permute-start(bf16[128,1024]{1,0:T(8,128)(2,1)S(1)} %get-tuple-element.68), channel_id=1, source_target_pairs={{0,2},{1,3},{2,0},{3,1},{4,6},{5,7},{6,4},{7,5},{8,10},{9,11},{10,... | collective-permute-start | bytes 786440 | tf_op jit(solution)/shard_map/ppermute | solution.py:101
  301.0 17.7 %collective-permute-start.35 = (bf16[256,1024]{1,0:T(8,128)(2,1)S(1)}, bf16[256,1024]{1,0:T(8,128)(2,1)S(1)}, u32[]{:S(2)}, u32[]{:S(2)}) collective-permute-start(bf16[256,1024]{1,0:T(8,128)(2,1)S(1)} %get-tuple-element.58), channel_id=1, source_target_pairs={{0,8},{4,12},{8,0},{12,4},{16,24},{20,28},{24,16},{28,20},{1,9},{5... | collective-permute-start | bytes 1572872 | tf_op jit(solution)/shard_map/ppermute | solution.py:49
  302.6 33.0 %collective-permute-start.37 = (bf16[256,1024]{1,0:T(8,128)(2,1)S(1)}, bf16[256,1024]{1,0:T(8,128)(2,1)S(1)}, u32[]{:S(2)}, u32[]{:S(2)}) collective-permute-start(bf16[256,1024]{1,0:T(8,128)(2,1)S(1)} %get-tuple-element.59), channel_id=1, source_target_pairs={{0,24},{4,28},{8,16},{12,20},{16,8},{20,12},{24,0},{28,4},{1,25},{... | collective-permute-start | bytes 1572872 | tf_op jit(solution)/shard_map/ppermute | solution.py:49
  303.1 32.5 %collective-permute-start.36 = (bf16[256,1024]{1,0:T(8,128)(2,1)S(1)}, bf16[256,1024]{1,0:T(8,128)(2,1)S(1)}, u32[]{:S(2)}, u32[]{:S(2)}) collective-permute-start(bf16[256,1024]{1,0:T(8,128)(2,1)S(1)} %get-tuple-element.60), channel_id=1, source_target_pairs={{0,16},{4,20},{8,24},{12,28},{16,0},{20,4},{24,8},{28,12},{1,17},{... | collective-permute-start | bytes 1572872 | tf_op jit(solution)/shard_map/ppermute | solution.py:49
  306.5 40.2 %collective-permute-start.23 = (bf16[256,1024]{1,0:T(8,128)(2,1)S(1)}, bf16[256,1024]{1,0:T(8,128)(2,1)S(1)}, u32[]{:S(2)}, u32[]{:S(2)}) collective-permute-start(bf16[256,1024]{1,0:T(8,128)(2,1)S(1)} %get-tuple-element.61), channel_id=1, source_target_pairs={{0,8},{4,12},{8,0},{12,4},{16,24},{20,28},{24,16},{28,20},{1,9},{5... | collective-permute-start | bytes 1572872 | tf_op jit(solution)/shard_map/ppermute | solution.py:49
  308.1 49.2 %collective-permute-start.25 = (bf16[256,1024]{1,0:T(8,128)(2,1)S(1)}, bf16[256,1024]{1,0:T(8,128)(2,1)S(1)}, u32[]{:S(2)}, u32[]{:S(2)}) collective-permute-start(bf16[256,1024]{1,0:T(8,128)(2,1)S(1)} %get-tuple-element.62), channel_id=1, source_target_pairs={{0,24},{4,28},{8,16},{12,20},{16,8},{20,12},{24,0},{28,4},{1,25},{... | collective-permute-start | bytes 1572872 | tf_op jit(solution)/shard_map/ppermute | solution.py:49
  318.7 39.9 %collective-permute-start.24 = (bf16[256,1024]{1,0:T(8,128)(2,1)S(1)}, bf16[256,1024]{1,0:T(8,128)(2,1)S(1)}, u32[]{:S(2)}, u32[]{:S(2)}) collective-permute-start(bf16[256,1024]{1,0:T(8,128)(2,1)S(1)} %get-tuple-element.63), channel_id=1, source_target_pairs={{0,16},{4,20},{8,24},{12,28},{16,0},{20,4},{24,8},{28,12},{1,17},{... | collective-permute-start | bytes 1572872 | tf_op jit(solution)/shard_map/ppermute | solution.py:49
  365.5 142.6 %all-gather.11.cloned.1.call-start = ((), (), s32[]{:S(2)}) async-start(), calls=%async_computation.3 | async-start | bytes 1769472 | tf_op jit(solution)/shard_map/all_gather | solution.py:444
  375.2 38.3 %collective-permute-start.48 = (bf16[4,4,32,1024]{3,2,1,0:T(8,128)(2,1)}, bf16[4,4,32,1024]{3,2,1,0:T(8,128)(2,1)}, u32[]{:S(2)}, u32[]{:S(2)}) collective-permute-start(bf16[4,4,32,1024]{3,2,1,0:T(8,128)(2,1)} %slice.203), channel_id=1, source_target_pairs={{0,4},{4,0},{8,12},{12,8},{16,20},{20,16},{24,28},{28,24},{1,5},{5... | collective-permute-start | bytes 3145736 | tf_op jit(solution)/shard_map/ppermute | solution.py:49
  406.2 56.6 %collective-permute-start.38 = (bf16[4,256,1024]{2,1,0:T(8,128)(2,1)}, bf16[4,256,1024]{2,1,0:T(8,128)(2,1)}, u32[]{:S(2)}, u32[]{:S(2)}) collective-permute-start(bf16[4,256,1024]{2,1,0:T(8,128)(2,1)} %slice.191), channel_id=1, source_target_pairs={{0,4},{4,0},{8,12},{12,8},{16,20},{20,16},{24,28},{28,24},{1,5},{5... | collective-permute-start | bytes 6291464 | tf_op jit(solution)/shard_map/ppermute | solution.py:49
  415.8 14.7 %collective-permute-start.46 = (bf16[256,384]{0,1:T(8,128)(2,1)S(1)}, bf16[256,384]{0,1:T(8,128)(2,1)S(1)}, u32[]{:S(2)}, u32[]{:S(2)}) collective-permute-start(bf16[256,384]{0,1:T(8,128)(2,1)S(1)} %bitcast.305), channel_id=1, source_target_pairs={{0,2},{1,3},{2,0},{3,1},{4,6},{5,7},{6,4},{7,5},{8,10},{9,11},{10,... | collective-permute-start | bytes 589832 | tf_op jit(solution)/shard_map/ppermute | solution.py:101
  417.4 37.8 %collective-permute-start.47 = (bf16[256,384]{0,1:T(8,128)(2,1)S(1)}, bf16[256,384]{0,1:T(8,128)(2,1)}, u32[]{:S(2)}, u32[]{:S(2)}) collective-permute-start(bf16[256,384]{0,1:T(8,128)(2,1)S(1)} %bitcast.304), channel_id=1, source_target_pairs={{0,3},{1,0},{2,1},{3,2},{4,7},{5,4},{6,5},{7,6},{8,11},{9,8},{10,9... | collective-permute-start | bytes 589832 | tf_op jit(solution)/shard_map/ppermute | solution.py:101
  420.4 36.6 %collective-permute-start.49 = (bf16[4,32,1024]{2,1,0:T(8,128)(2,1)S(1)}, bf16[4,32,1024]{2,1,0:T(8,128)(2,1)S(1)}, u32[]{:S(2)}, u32[]{:S(2)}) collective-permute-start(bf16[4,32,1024]{2,1,0:T(8,128)(2,1)S(1)} %get-tuple-element.72), channel_id=1, source_target_pairs={{0,8},{4,12},{8,0},{12,4},{16,24},{20,28},{24,16},{28,20},{1,9},{5... | collective-permute-start | bytes 786440 | tf_op jit(solution)/shard_map/ppermute | solution.py:49
  423.3 33.7 %collective-permute-start.51 = (bf16[4,32,1024]{2,1,0:T(8,128)(2,1)S(1)}, bf16[4,32,1024]{2,1,0:T(8,128)(2,1)S(1)}, u32[]{:S(2)}, u32[]{:S(2)}) collective-permute-start(bf16[4,32,1024]{2,1,0:T(8,128)(2,1)S(1)} %get-tuple-element.73), channel_id=1, source_target_pairs={{0,24},{4,28},{8,16},{12,20},{16,8},{20,12},{24,0},{28,4},{1,25},{... | collective-permute-start | bytes 786440 | tf_op jit(solution)/shard_map/ppermute | solution.py:49
  430.5 26.5 %collective-permute-start.50 = (bf16[4,32,1024]{2,1,0:T(8,128)(2,1)S(1)}, bf16[4,32,1024]{2,1,0:T(8,128)(2,1)S(1)}, u32[]{:S(2)}, u32[]{:S(2)}) collective-permute-start(bf16[4,32,1024]{2,1,0:T(8,128)(2,1)S(1)} %get-tuple-element.74), channel_id=1, source_target_pairs={{0,16},{4,20},{8,24},{12,28},{16,0},{20,4},{24,8},{28,12},{1,17},{... | collective-permute-start | bytes 786440 | tf_op jit(solution)/shard_map/ppermute | solution.py:49
  459.5 31.1 %collective-permute-start.54 = (bf16[32,1024]{1,0:T(8,128)(2,1)}, bf16[32,1024]{1,0:T(8,128)(2,1)}, u32[]{:S(2)}, u32[]{:S(2)}) collective-permute-start(bf16[32,1024]{1,0:T(8,128)(2,1)} %get-tuple-element.86), channel_id=1, source_target_pairs={{0,3},{1,0},{2,1},{3,2},{4,7},{5,4},{6,5},{7,6},{8,11},{9,8},{10,9... | collective-permute-start | bytes 196616 | tf_op jit(solution)/shard_map/ppermute | solution.py:101
  462.3 28.4 %collective-permute-start.53 = (bf16[32,1024]{1,0:T(8,128)(2,1)}, bf16[32,1024]{1,0:T(8,128)(2,1)}, u32[]{:S(2)}, u32[]{:S(2)}) collective-permute-start(bf16[32,1024]{1,0:T(8,128)(2,1)} %get-tuple-element.87), channel_id=1, source_target_pairs={{0,2},{1,3},{2,0},{3,1},{4,6},{5,7},{6,4},{7,5},{8,10},{9,11},{10,... | collective-permute-start | bytes 196616 | tf_op jit(solution)/shard_map/ppermute | solution.py:101
  466.5 36.6 %collective-permute-start.39 = (bf16[256,1024]{1,0:T(8,128)(2,1)}, bf16[256,1024]{1,0:T(8,128)(2,1)S(1)}, u32[]{:S(2)}, u32[]{:S(2)}) collective-permute-start(bf16[256,1024]{1,0:T(8,128)(2,1)} %get-tuple-element.55), channel_id=1, source_target_pairs={{0,8},{4,12},{8,0},{12,4},{16,24},{20,28},{24,16},{28,20},{1,9},{5... | collective-permute-start | bytes 1572872 | tf_op jit(solution)/shard_map/ppermute | solution.py:49
  466.5 36.6 %collective-permute-start.41 = (bf16[256,1024]{1,0:T(8,128)(2,1)}, bf16[256,1024]{1,0:T(8,128)(2,1)}, u32[]{:S(2)}, u32[]{:S(2)}) collective-permute-start(bf16[256,1024]{1,0:T(8,128)(2,1)} %get-tuple-element.56), channel_id=1, source_target_pairs={{0,24},{4,28},{8,16},{12,20},{16,8},{20,12},{24,0},{28,4},{1,25},{... | collective-permute-start | bytes 1572872 | tf_op jit(solution)/shard_map/ppermute | solution.py:49
  469.0 34.1 %collective-permute-start.40 = (bf16[256,1024]{1,0:T(8,128)(2,1)}, bf16[256,1024]{1,0:T(8,128)(2,1)}, u32[]{:S(2)}, u32[]{:S(2)}) collective-permute-start(bf16[256,1024]{1,0:T(8,128)(2,1)} %get-tuple-element.57), channel_id=1, source_target_pairs={{0,16},{4,20},{8,24},{12,28},{16,0},{20,4},{24,8},{28,12},{1,17},{... | collective-permute-start | bytes 1572872 | tf_op jit(solution)/shard_map/ppermute | solution.py:49
  (47 other events, 419.9 us)
Sparse Core Ops, SparseCore 0:
  34.9 80.2 all-gather.8
  249.7 31.1 all-gather.12
  298.4 43.6 all-gather.14
  457.1 41.0 all-gather.10
